TPU v7x, 32 devices: a whole 2x2x4 slice. The times are simulated.
32 devices in a mesh: xy: 16 (over z, x, core), gz: 2 (over y).
Axes of the slice: x: 2, y: 2, z: 4, core: 2. Of those that a mesh axis runs over, the one named last changes fastest.
Arguments:
- field_tiles: bfloat16 [16, 128, 128, 256], P('xy', None, None, 'gz'), may hold values from -6 to 6
- core_x: bfloat16 [512, 192], replicated, may hold values from -0.25 to 0.25
- core_y: bfloat16 [512, 192], replicated, may hold values from -0.25 to 0.25
- core_z: bfloat16 [256, 192], P('gz'), may hold values from -0.375 to 0.375
- x_second: bfloat16 [512, 96], replicated, may hold values from -0.25 to 0.25
- x_third: bfloat16 [512, 96], replicated, may hold values from -0.25 to 0.25
- y_first: bfloat16 [512, 96], replicated, may hold values from -0.25 to 0.25
- y_third: bfloat16 [512, 96], replicated, may hold values from -0.25 to 0.25
- z_first: bfloat16 [256, 96], P('gz'), may hold values from -0.375 to 0.375
- z_second: bfloat16 [256, 96], P('gz'), may hold values from -0.375 to 0.375
Outputs:
- mode_one: float32 [512, 96], P(('xy', 'gz'))
- mode_two: float32 [512, 96], P(('xy', 'gz'))
- mode_three: float32 [96, 256], P('xy', 'gz')
- core_sketch: float32 [192, 192, 192], P('xy', None, 'gz')
All inputs are finite; a program needn't handle non-finite values.
Results may differ from a plain program's by a relative error of at most 0.007.
Values may be sent and summed in bfloat16 or wider, within the bound.
No kernel may reach another device: no remote copies, remote signals or barrier semaphores. Data moves between devices by JAX's collectives and lax.ppermute only.
A program may use at most 128 MiB of HBM per device.

v0:
```python
import jax
import jax.numpy as jnp
from jax import lax
from jax.sharding import PartitionSpec as P

K = 96
TX = 128
TY = 128


def row_slice(matrix, offset, length):
    return lax.dynamic_slice_in_dim(matrix, offset, length, 0)


def shards(
    field_tiles, core_x, core_y, core_z, x_second, x_third, y_first, y_third, z_first, z_second
):
    tile_total = lax.axis_size("xy")
    column_tiles = tile_total // 4
    tile_index = lax.axis_index("xy")
    x_offset = tile_index // column_tiles * TX
    y_offset = tile_index % column_tiles * TY
    block_data = field_tiles[0]
    z_pair = jnp.concatenate([z_first, z_second], axis=1)
    paired = jnp.einsum("abz,zk->abk", block_data, z_pair, preferred_element_type=jnp.float32)
    g_one = jnp.sum(
        paired[:, :, :K] * row_slice(y_first, y_offset, TY).astype(jnp.float32)[None], axis=1
    )
    g_two = jnp.sum(
        paired[:, :, K:] * row_slice(x_second, x_offset, TX).astype(jnp.float32)[:, None], axis=0
    )
    first_full = lax.dynamic_update_slice_in_dim(
        jnp.zeros((x_second.shape[0], K), jnp.float32), g_one, x_offset, 0
    )
    second_full = lax.dynamic_update_slice_in_dim(
        jnp.zeros((y_first.shape[0], K), jnp.float32), g_two, y_offset, 0
    )
    mode_one, mode_two = (
        lax.psum_scatter(first_full, ("xy", "gz"), scatter_dimension=0, tiled=True),
        lax.psum_scatter(second_full, ("xy", "gz"), scatter_dimension=0, tiled=True),
    )
    across = jnp.einsum(
        "abz,ak->bkz",
        block_data,
        row_slice(x_third, x_offset, TX),
        preferred_element_type=jnp.float32,
    )
    g_three = jnp.sum(
        across * row_slice(y_third, y_offset, TY).astype(jnp.float32)[:, :, None], axis=0
    )
    mode_three = lax.psum_scatter(g_three, "xy", scatter_dimension=0, tiled=True)
    z_matrix = core_z.astype(jnp.float32)
    lowered = jnp.einsum(
        "abz,ap->pbz",
        block_data,
        row_slice(core_x, x_offset, TX),
        preferred_element_type=jnp.float32,
    ).astype(jnp.bfloat16)
    y_rows = row_slice(core_y, y_offset, TY)
    plane_part = lax.psum_scatter(
        jnp.einsum("pbz,bq->pqz", lowered, y_rows, preferred_element_type=jnp.float32),
        "xy",
        scatter_dimension=0,
        tiled=True,
    )
    partial_value = jnp.einsum("pqz,zr->pqr", plane_part, z_matrix, precision=lax.Precision.HIGHEST)
    core_sketch = lax.psum_scatter(partial_value, "gz", scatter_dimension=2, tiled=True)
    return (mode_one, mode_two, mode_three, core_sketch)


def solution(mesh):
    return jax.shard_map(
        shards,
        mesh=mesh,
        in_specs=(
            P("xy", None, None, "gz"),
            P(),
            P(),
            P("gz", None),
            P(),
            P(),
            P(),
            P(),
            P("gz", None),
            P("gz", None),
        ),
        out_specs=(
            P(("xy", "gz"), None),
            P(("xy", "gz"), None),
            P("xy", "gz"),
            P("xy", None, "gz"),
        ),
        check_vma=False,
    )
```

profile of v0, /device:TPU:0, one launch (start us, length us, event | category | flops | bytes accessed | tf_op | source)
XLA Modules:
  0.0 539.8 jit_solution(8032309325866016523)
XLA Ops:
  7.2 0.0 copy-start
  7.2 0.0 reduce-scatter.11.cloned.1.call-start
  7.3 5.9 %fusion.3 = bf16[192,128,128]{2,0,1:T(8,128)(2,1)S(1)} fusion(bf16[128,128,128]{2,1,0:T(8,128)(2,1)} %bitcast.30, bf16[512,192]{0,1:T(8,128)(2,1)} %param.11, s32[]{:T(128)S(6)} %select_n.26), kind=kOutput, calls=%fused_computation.9 | convolution fusion | flops 805306368 | bytes 10534916 | tf_op jit(solution)/shard_map/abz,ap->pbz/dot_general | solution.py:53
  13.1 0.0 copy-done
  13.1 17.7 %convolution_bitcast_fusion = f32[192,192,128]{2,1,0:T(8,128)} fusion(bf16[192,128,128]{2,0,1:T(8,128)(2,1)S(1)} %fusion.3, bf16[512,192]{0,1:T(8,128)(2,1)S(1)} %copy-done, s32[]{:T(128)S(6)} %select_n.24), kind=kOutput, calls=%fused_computation.1 | convolution fusion | flops 1207959552 | bytes 25214980 | tf_op jit(solution)/shard_map/pbz,bq->pqz/dot_general | solution.py:61
  30.8 0.0 copy-start.3
  30.8 0.0 reduce-scatter.11.cloned.1.call-update
  30.8 0.2 reduce-scatter.13.cloned.1.call-start
  31.1 197.4 %reduce-scatter.11.cloned.1.call-done = f32[12,192,128]{2,1,0:T(8,128)} async-done(((f32[192,192,128]{2,1,0:T(8,128)}), f32[12,192,128]{2,1,0:T(8,128)}) %reduce-scatter.11.cloned.1.call-update) | async-done | bytes 1179664 | tf_op jit(solution)/shard_map/reduce_scatter | solution.py:60
  228.4 0.0 copy-done.3
  228.4 3.8 fusion.11
  232.2 3.1 copy.22
  235.3 0.0 copy-start.4
  235.3 0.0 copy-start.5
  235.4 2.0 reshape.16
  237.3 0.0 reduce-scatter.13.cloned.1.call-update
  237.3 0.0 reduce-scatter.9.cloned.1.call-start
  237.4 0.7 dynamic-slice_convert_fusion.1
  238.1 0.1 copy.17
  238.2 0.7 dynamic-slice_convert_fusion.2
  239.0 0.0 copy-done.4
  239.0 0.0 copy-done.5
  239.0 4.0 convolution_bitcast_fusion.1
  243.0 0.0 copy-start.6
  243.0 4.2 fusion
  247.2 0.1 copy.18
  247.4 0.0 copy-start.2
  247.4 0.7 copy-done.2
  248.1 0.0 reduce-scatter.9.cloned.1.call-update
  248.1 0.0 reduce-scatter.7.cloned.1.call-start
  248.2 0.0 copy-start.1
  248.2 0.7 copy-done.1
  248.9 0.0 reduce-scatter.7.cloned.1.call-update
  249.0 0.7 dynamic-slice_convert_fusion
  249.7 0.1 copy.20
  249.8 0.0 copy-done.6
  249.8 0.6 dynamic-slice
  251.1 6.1 %fusion.2 = f32[96,128]{1,0:T(8,128)S(1)} fusion(f32[128,96]{1,0:T(8,128)S(1)} %copy.20, bf16[128,128,128]{2,1,0:T(8,128)(2,1)} %bitcast.31, bf16[512,96]{0,1:T(8,128)(2,1)} %param.15, s32[]{:T(128)S(6)} %select_n.26), kind=kOutput, calls=%fused_computation.7 | convolution fusion | flops 405786624 | bytes 4317188 | tf_op jit(solution)/shard_map/abz,ak->bkz/dot_general | solution.py:42
  257.1 59.7 %all-reduce = f32[96,128]{1,0:T(8,128)S(1)} all-reduce(f32[96,128]{1,0:T(8,128)S(1)} %fusion.2), channel_id=4, replica_groups=mesh['xy'=16,'gz'=2] {'xy'}, use_global_device_ids=true, to_apply=%region_5.6.clone | all-reduce | flops 12288 | bytes 98304
  316.9 0.6 constant_dynamic-slice_fusion
  317.5 0.0 reduce-scatter.13.cloned.1.call-done
  317.5 1.9 reshape.17
  319.3 1.8 copy.23
  321.1 80.1 %reduce-scatter.9.cloned.1.call-done = f32[16,96]{1,0:T(8,128)} async-done(((f32[512,96]{1,0:T(8,128)}), f32[16,96]{1,0:T(8,128)}) %reduce-scatter.9.cloned.1.call-update) | async-done | bytes 6160 | tf_op jit(solution)/shard_map/reduce_scatter | solution.py:40
  401.2 132.0 %reduce-scatter.7.cloned.1.call-done = f32[16,96]{1,0:T(8,128)} async-done(((f32[512,96]{1,0:T(8,128)}), f32[16,96]{1,0:T(8,128)}) %reduce-scatter.7.cloned.1.call-update) | async-done | bytes 6160 | tf_op jit(solution)/shard_map/reduce_scatter | solution.py:39
  (4 shorter events, 0.1 us)
Async XLA Ops:
  7.2 6.0 %copy-start = (bf16[512,192]{0,1:T(8,128)(2,1)S(1)}, bf16[512,192]{0,1:T(8,128)(2,1)}, u32[]{:S(2)}) copy-start(bf16[512,192]{0,1:T(8,128)(2,1)} %param.12) | copy-start | bytes 589828
  7.2 221.3 %reduce-scatter.11.cloned.1.call-start = ((), (), s32[]{:S(2)}) async-start(), calls=%async_computation.6 | async-start | bytes 20054016 | tf_op jit(solution)/shard_map/reduce_scatter | solution.py:60
  30.8 197.6 %copy-start.3 = (bf16[128,192]{0,1:T(8,128)(2,1)S(1)}, bf16[128,192]{0,1:T(8,128)(2,1)}, u32[]{:S(2)}) copy-start(bf16[128,192]{0,1:T(8,128)(2,1)} %param.13) | copy-start | bytes 147460
  30.8 286.6 %reduce-scatter.13.cloned.1.call-start = ((), (), s32[]{:S(2)}) async-start(), calls=%async_computation.7 | async-start | bytes 2654208
  235.3 3.7 copy-start.4
  235.3 3.6 copy-start.5
  237.3 163.9 %reduce-scatter.9.cloned.1.call-start = ((), (), s32[]{:S(2)}) async-start(), calls=%async_computation.5 | async-start | bytes 270336 | tf_op jit(solution)/shard_map/reduce_scatter | solution.py:40
  243.0 6.8 %copy-start.6 = (u32[32]{0:T(128)S(1)}, u32[32]{0:T(128)}, u32[]{:S(2)}) copy-start(u32[32]{0:T(128)} %constant.43) | copy-start | bytes 388
  247.4 0.7 copy-start.2
  248.1 285.1 %reduce-scatter.7.cloned.1.call-start = ((), (), s32[]{:S(2)}) async-start(), calls=%async_computation.4 | async-start | bytes 270336 | tf_op jit(solution)/shard_map/reduce_scatter | solution.py:39
  248.2 0.7 copy-start.1
Sparse Core Ops, SparseCore 0:
  30.9 197.4 reduce-scatter.10
  237.5 27.3 reduce-scatter.12
  267.8 133.4 reduce-scatter.8
  403.9 129.3 reduce-scatter.6
where the time goes:
time: 540 us
  waiting for transfers between devices  410 us (76%)
  blocking collectives  59.7 us (11%)
  matrix products  37.4 us (7%)
  between operations  14.6 us (3%)
  local copies, waits for them, and re-layouts  11.7 us (2%)
  other arithmetic  6.47 us (1%)
    reduce_scatter x1, waiting for transfers between devices, shards(): lax.psum_scatter(jnp.einsum('pbz,bq->pqz', lowered, y_rows, preferred_ele...  197 us
    reduce_scatter x1, waiting for transfers between devices, shards(): lax.psum_scatter(first_full, ('xy', 'gz'), scatter_dimension=0, tiled=True)  132 us
    reduce_scatter x1, waiting for transfers between devices, shards(): lax.psum_scatter(second_full, ('xy', 'gz'), scatter_dimension=0, tiled=True)  80.1 us
    unnamed x1, blocking collectives  59.7 us
    dot_general x1, matrix products, shards(): jnp.einsum('pbz,bq->pqz', lowered, y_rows, preferred_element_type=jnp.flo...  17.7 us
    unnamed x20, local copies, waits for them, and re-layouts  11.3 us
  transfers between devices with their start and end apart: 4, of which 3 were waited for; matrix products, arithmetic and copies ran while one was open for 4% of the time, Pallas kernels for 0%

commit v1 on v0

v1 whole, which is shorter than its diff:
```python
import functools

import jax
import jax.numpy as jnp
from jax import lax
from jax.experimental import pallas as pl
from jax.experimental.pallas import tpu as pltpu
from jax.sharding import PartitionSpec as P

TX = 128
TY = 128
LANES = 128
REGIONS = 8
ROWS = 32
UNIT = 8
PLAN = (1, 1, 1, 1, 1, 1)
PAIR_PLAN = (1, 1, 1, 1, 1, 1)
RIDING = 1
EARLY = 3
WAIT = 0
LAG = 3.1
PACK = 4
F32 = jnp.float32
BF16 = jnp.bfloat16


def dot(a, b):
    return jnp.dot(a, b, preferred_element_type=F32)


def cut(matrix, offset, length, axis):
    return lax.dynamic_slice_in_dim(matrix, offset, length, axis)


def modes_kernel(
    tile, low, high, z_first, z_second, y_one, x_two, y_three, x_three, one, two, three, z_pair, ones, twos, x_parts
):
    del tile
    step, rows = pl.program_id(0), 2 * low.shape[0]
    k = y_three.shape[0]

    @pl.when(step == 0)
    def _():
        two[...] = jnp.zeros_like(two)
        three[...] = jnp.zeros_like(three)
        for ref in (z_pair, ones, twos):
            ref[...] = jnp.zeros_like(ref)
        z_pair[:, :k] = z_first[...].astype(F32).T.astype(BF16)
        z_pair[:, LANES : LANES + k] = z_second[...].astype(F32).T.astype(BF16)
        ones[:, :k] = y_one[...].astype(F32).T
        twos[:, :k] = x_two[...].astype(F32).T
        for n in range(x_parts.shape[0]):
            x_parts[n] = x_three[...].astype(F32)[:, n * rows : (n + 1) * rows]

    sum_two = jnp.zeros(two.shape, F32)
    sum_three = jnp.zeros(three.shape, F32)
    for i in range(rows):
        plane = (low, high)[i * 2 // rows][i % low.shape[0]]
        paired = dot(plane, z_pair[...])
        one[i : i + 1, :] = jnp.sum(paired[:, :LANES] * ones[...], axis=0, keepdims=True)
        sum_two += paired[:, LANES:] * twos[pl.ds(step * rows + i, 1), :]
        sum_three += dot(y_three[...], plane) * x_parts[step, :, i : i + 1]
    two[...] += sum_two
    three[...] += sum_three


def modes(tile, field, z_first, z_second, y_first, x_second, y_third, x_third):
    tx, ty, nz = field.shape
    k = z_first.shape[1]
    steps = tx // ROWS
    whole = lambda *shape: pl.BlockSpec(shape, lambda i, tile: (0,) * len(shape))
    row = pl.BlockSpec((k, tx), lambda i, tile: (0, tile[0]))
    column = pl.BlockSpec((k, ty), lambda i, tile: (0, tile[1]))
    return pl.pallas_call(
        modes_kernel,
        grid_spec=pltpu.PrefetchScalarGridSpec(
            num_scalar_prefetch=1,
            grid=(steps,),
            in_specs=[
                pl.BlockSpec((ROWS // 2, ty, nz), lambda i, tile: (2 * i, 0, 0)),
                pl.BlockSpec((ROWS // 2, ty, nz), lambda i, tile: (2 * i + 1, 0, 0)),
                whole(k, nz),
                whole(k, nz),
                column,
                row,
                column,
                row,
            ],
            out_specs=[
                pl.BlockSpec((ROWS, LANES), lambda i, tile: (i, 0)),
                whole(ty, LANES),
                whole(k, nz),
            ],
            scratch_shapes=[
                pltpu.VMEM((nz, 2 * LANES), BF16),
                pltpu.VMEM((ty, LANES), F32),
                pltpu.VMEM((tx, LANES), F32),
                pltpu.VMEM((steps, k, ROWS), F32),
            ],
        ),
        out_shape=[
            jax.ShapeDtypeStruct((tx, LANES), F32),
            jax.ShapeDtypeStruct((ty, LANES), F32),
            jax.ShapeDtypeStruct((k, nz), F32),
        ],
        compiler_params=pltpu.CompilerParams(vmem_limit_bytes=56 << 20),
        cost_estimate=pl.CostEstimate(
            flops=2 * tx * ty * nz * (2 * LANES + k), bytes_accessed=2 * tx * ty * nz, transcendentals=0
        ),
        name="modes",
    )(tile, field, field, z_first.T, z_second.T, y_first.T, x_second.T, y_third.T, x_third.T)


def plane_kernel(targets, place, low, high, other_low, other_high, own, sibling, *refs):
    outs, maps, rows = refs[:-2], refs[-2], refs[-1]

    @pl.when(pl.program_id(0) == 0)
    def _():
        share = maps.shape[0] // targets
        rows[:, :TY] = own[...].astype(F32)
        rows[:, TY:] = sibling[...].astype(F32)
        for j in range(targets):
            here = pl.ds(pl.multiple_of(place[3 + j] * share, 8), share)
            for n in range(2):
                maps[j * share : (j + 1) * share, n * TY : (n + 1) * TY] = rows[here, n * TY : (n + 1) * TY]

    held = maps[...].astype(BF16)
    half = low.shape[0]
    for i in range(0, 2 * half, 2):
        field, other = ((low, other_low), (high, other_high))[i // half]
        pair = [jnp.concatenate([field[k], other[k]], axis=0) for k in (i % half, i % half + 1)]
        result = dot(held, jnp.concatenate(pair, axis=1))
        nz = result.shape[1] // 2
        at = 0
        for out in outs:
            block = result[at : at + out.shape[1]].astype(out.dtype)
            out[i] = block[:, :nz]
            out[i + 1] = block[:, nz:]
            at += out.shape[1]


def plane(place, field, other, y_map, counts):
    tx, ty, nz = field.shape
    targets, size = place.shape[0] - 3, y_map.shape[0]
    low = pl.BlockSpec((ROWS // 2, ty, nz), lambda i, place: (2 * i, 0, 0))
    high = pl.BlockSpec((ROWS // 2, ty, nz), lambda i, place: (2 * i + 1, 0, 0))
    kinds = [(count, BF16) for count in counts] * targets
    return pl.pallas_call(
        functools.partial(plane_kernel, targets),
        grid_spec=pltpu.PrefetchScalarGridSpec(
            num_scalar_prefetch=1,
            grid=(tx // ROWS,),
            in_specs=[
                low,
                high,
                low,
                high,
                pl.BlockSpec((size, ty), lambda i, place: (0, place[1])),
                pl.BlockSpec((size, ty), lambda i, place: (0, place[2])),
            ],
            out_specs=[pl.BlockSpec((ROWS, count, nz), lambda i, place: (i, 0, 0)) for count, _ in kinds],
            scratch_shapes=[
                pltpu.VMEM((targets * sum(counts), 2 * ty), F32),
                pltpu.VMEM((size, 2 * ty), F32),
            ],
        ),
        out_shape=[jax.ShapeDtypeStruct((tx, count, nz), kind) for count, kind in kinds],
        compiler_params=pltpu.CompilerParams(vmem_limit_bytes=56 << 20),
        cost_estimate=pl.CostEstimate(
            flops=4 * tx * ty * nz * targets * sum(counts), bytes_accessed=6 * tx * ty * nz, transcendentals=0
        ),
        name="plane",
    )(place, field, field, other, other, y_map, y_map)


def along_z_kernel(slabs, pack, extras, first, count, near, *refs):
    far, z_map, rows = refs[: -slabs - extras - 2], refs[-slabs - extras - 2], refs[-1]
    added, outs = refs[-slabs - extras - 1 : -slabs - 1], refs[-slabs - 1 : -1]
    tx, _, nz = near.shape
    total = near[...].astype(F32)
    for ref in far:
        total += ref[...].astype(F32)
    total = total[:, first : first + count]
    rows[...] = total.reshape(tx * count, nz)
    width = z_map.shape[1] // slabs
    at = 0
    for g in range(count // pack):
        parts = [rows[pl.ds(g * pack + i, tx, stride=count), :] for i in range(pack)]
        result = dot(jnp.concatenate(parts, axis=1).astype(BF16), z_map[...])
        for t in range(width // LANES):
            for s, out in enumerate(outs):
                block = result[:, s * width + t * LANES : s * width + (t + 1) * LANES]
                out[at : at + tx, :] = block.astype(out.dtype)
            at += tx
    for extra in added:
        for out in outs:
            out[at : at + extra.shape[0], :] = extra[...].astype(out.dtype)
        at += extra.shape[0]


def along_z(near, far, first, count, z_map, slabs, pack, added):
    tx, _, nz = near.shape
    rows = tx * (count // pack) * (z_map.shape[1] // slabs // LANES) + sum(x.shape[0] for x in added)
    return pl.pallas_call(
        functools.partial(along_z_kernel, slabs, pack, len(added), first, count),
        out_shape=[jax.ShapeDtypeStruct((rows, LANES), BF16 if s else F32) for s in range(slabs)],
        scratch_shapes=[pltpu.VMEM((tx * count, nz), F32)],
        compiler_params=pltpu.CompilerParams(vmem_limit_bytes=16 << 20),
        cost_estimate=pl.CostEstimate(
            flops=2 * tx * count // pack * z_map.shape[0] * z_map.shape[1],
            bytes_accessed=8 * tx * count * nz,
            transcendentals=0,
        ),
        name="along_z",
    )(near, *far, z_map, *added)


def along_x_kernel(tall, riders, near, *refs):
    outs = refs[-2 - riders :]
    far, (x_map, *three) = refs[: -4 - 2 * riders + 1], refs[-4 - 2 * riders + 1 : -2 - riders]
    tx = x_map.shape[1]
    piece = x_map.shape[0] // REGIONS

    def total(at, rows):
        found = near[at : at + rows, :]
        for ref in far:
            found += ref[at : at + rows, :].astype(F32)
        return found

    tiles = tall // tx
    for t in range(0, tiles, 2):
        results = [dot(x_map[...], total(at, tx).astype(BF16)) for at in (t * tx, (t + 1) * tx)]
        for r in range(REGIONS):
            block = jnp.concatenate([x[r * piece : (r + 1) * piece] for x in results], axis=0)
            out = outs[r * 2 // REGIONS]
            at = (r % (REGIONS // 2) * tiles + t) * piece
            out[at : at + 2 * piece, :] = block.astype(out.dtype)
    if riders:
        at = REGIONS // 2 * tiles * piece
        outs[2][...] = total(tall, TX)
        two = total(tall + TX, TY)
        for out in outs[:2]:
            out[at : at + TY, :] = two.astype(out.dtype)
            out[at + TY :, :] = three[0][...].astype(out.dtype)


def along_x(near, far, x_map, tall, riders):
    rows = tall // x_map.shape[1] * x_map.shape[0] // 2
    shapes = [(rows, F32), (rows, BF16)]
    if riders:
        rows += TY + riders[0].shape[0]
        shapes = [(rows, F32), (rows, BF16), (TX, F32)]
    return pl.pallas_call(
        functools.partial(along_x_kernel, tall, len(riders)),
        out_shape=[jax.ShapeDtypeStruct((n, LANES), kind) for n, kind in shapes],
        compiler_params=pltpu.CompilerParams(vmem_limit_bytes=16 << 20),
        cost_estimate=pl.CostEstimate(
            flops=2 * tall * x_map.shape[0] * LANES, bytes_accessed=6 * tall * LANES, transcendentals=0
        ),
        name="along_x",
    )(near, *far, x_map, *riders)


def add_split_kernel(half, shared, near, far, *outs):
    for n, out in enumerate(outs[:2]):
        out[:half, :] = (near[n * half : (n + 1) * half, :] + far[n * half : (n + 1) * half, :]).astype(out.dtype)
    rest = near[2 * half :, :] + far[2 * half :, :] if near.shape[0] > 2 * half else None
    if rest is not None and shared:
        for out in outs:
            out[half:, :] = rest.astype(out.dtype)
    elif rest is not None:
        outs[2][...] = rest


def add_split(near, far, half, shared):
    rest = near.shape[0] - 2 * half
    rows = half + rest * shared
    shapes = [(rows, F32), (rows, BF16)] + ([(rest, F32)] if rest and not shared else [])
    return pl.pallas_call(
        functools.partial(add_split_kernel, half, shared),
        out_shape=[jax.ShapeDtypeStruct((n, LANES), kind) for n, kind in shapes],
        compiler_params=pltpu.CompilerParams(vmem_limit_bytes=16 << 20),
        cost_estimate=pl.CostEstimate(
            flops=near.size, bytes_accessed=9 * near.size, transcendentals=0
        ),
        name="add_split",
    )(near, far)


def unpack_kernel(counts, pack, width, columns, column, sketches, *refs):
    groups, modes, out, rows, flat = refs[: len(counts)], refs[-6:-3], refs[-3], refs[-2], refs[-1]
    p_rows, s_size, z_size = out.shape
    at = 0
    for mode in modes:
        height, wide = mode.shape
        mode[...] = sketches[pl.ds(at + column[0] * height, height), :][:, :wide]
        at += columns * height
    low = columns // 2
    half = low * p_rows
    first = 0
    for pieces, group in zip(groups, counts):
        size = pieces.shape[0] // columns
        rows[: pieces.shape[0], :] = pieces[...].astype(F32)
        for d in range(columns):
            source = (reverse_bits(d % low, low) * 2 + d // low) * size
            q = first
            for count in group:
                for g in range(count // pack):
                    wide = jnp.concatenate(
                        [
                            rows[source + t * half : source + (t + 1) * half, :]
                            for t in range(width // LANES)
                        ],
                        axis=1,
                    )
                    source += half * (width // LANES)
                    for i in range(pack):
                        at = (g * pack + i) * half
                        flat[at : at + half, :z_size] = wide[:, i * z_size : (i + 1) * z_size]
                start = pl.multiple_of((column[0] ^ d) * (s_size // columns) + q, UNIT)
                for p in range(p_rows):
                    found = flat[pl.ds(d % low * p_rows + p, count, stride=half), :]
                    out[p, pl.ds(start, count), :] = found[:, :z_size]
                q += count
        first += sum(group)


def unpack(groups, counts, sketches, column, shapes, sizes):
    pack, width, columns = sizes
    half = columns // 2 * shapes[-1][0]
    vmem = pl.BlockSpec(memory_space=pltpu.VMEM)
    return pl.pallas_call(
        functools.partial(unpack_kernel, counts, pack, width, columns),
        in_specs=[pl.BlockSpec(memory_space=pltpu.SMEM)] + [vmem] * (1 + len(groups)),
        out_specs=[vmem] * len(shapes),
        out_shape=[jax.ShapeDtypeStruct(shape, F32) for shape in shapes],
        scratch_shapes=[
            pltpu.VMEM((max(x.shape[0] for x in groups), LANES), F32),
            pltpu.VMEM((max(sum(counts, [])) * half, LANES), F32),
        ],
        compiler_params=pltpu.CompilerParams(vmem_limit_bytes=16 << 20),
        cost_estimate=pl.CostEstimate(
            flops=4 * groups[0].size, bytes_accessed=8 * groups[0].size, transcendentals=0
        ),
        name="unpack",
    )(column.reshape(1).astype(jnp.int32), sketches, *groups)


def reverse_bits(value, size):
    bits = size.bit_length() - 1
    return sum(((value >> n) & 1) << (bits - 1 - n) for n in range(bits))


def after(token, *values):
    return lax.optimization_barrier((token, *values))[1:]


def shards(
    field_tiles, core_x, core_y, core_z, x_second, x_third, y_first, y_third, z_first, z_second
):
    tiles, slabs = lax.axis_size("xy"), lax.axis_size("gz")
    row_tiles = core_x.shape[0] // TX
    column_tiles = tiles // row_tiles
    pairs = column_tiles // 2
    me, slab = lax.axis_index("xy"), lax.axis_index("gz")
    u, v = me // column_tiles, me % column_tiles
    side, pair = v % 2, v // 2
    s_size, k = core_x.shape[1], x_third.shape[1]
    field = field_tiles[0]
    nz = field.shape[2]
    share = s_size // column_tiles
    units = share // UNIT
    counts = [UNIT * n for n in (PLAN if sum(PLAN) == units else [1] * units)]
    chunks = len(counts)
    riding = min(RIDING, chunks - 1)
    groups = PAIR_PLAN if sum(PAIR_PLAN) == chunks else [1] * chunks
    place = [(g, n) for g, size in enumerate(groups) for n in range(size)]
    starts = [sum(counts[c - n : c]) for c, (_, n) in enumerate(place)]
    wides = [sum(counts[c] for c in range(chunks) if place[c][0] == g) for g in range(len(groups))]
    early = min(max(EARLY, riding + 1), chunks - 1)
    z_size = s_size // slabs
    p_size = s_size // row_tiles
    p_rows = s_size // tiles
    pack = PACK if PACK * z_size % LANES == 0 else UNIT
    width = -(-pack * z_size // LANES) * LANES
    one_rows = core_x.shape[0] // (tiles * slabs)
    two_rows = core_y.shape[0] // (tiles * slabs)
    three_rows = k // tiles

    def flip(x, bit):
        return lax.ppermute(x, "xy", [(i, i ^ bit) for i in range(tiles)])

    def to_pair(x, step):
        def target(i):
            row, column = divmod(i, column_tiles)
            return row * column_tiles + (column // 2 + step) % pairs * 2 + column % 2

        return lax.ppermute(x, "xy", [(i, target(i)) for i in range(tiles)])

    def to_slab(x, step):
        if step == 0:
            return x
        return lax.ppermute(x, "gz", [(i, (i + step) % slabs) for i in range(slabs)])

    other = flip(field, 1)
    owners = [(pair + j) % pairs * 2 + side for j in range(pairs)]
    columns = jnp.stack([u, v, v + 1 - 2 * side, *owners]).astype(jnp.int32)
    one, two, three = modes(columns, field, z_first, z_second, y_first, x_second, y_third, x_third)
    (columns,) = after(one, columns)
    parts = plane(columns, field, other, core_y.T, wides)
    core_x, core_z = after(parts[0], core_x, core_z)
    arrived = [
        [to_pair(parts[j * len(wides) + g], j) for j in range(1, pairs)] for g in range(len(wides))
    ]

    z_map = []
    for step in range(slabs):
        block = cut(core_z, (slab + step) % slabs * z_size, z_size, 1)
        block = jnp.eye(pack, dtype=BF16)[:, None, :, None] * block[None, :, None, :]
        block = block.reshape(pack * nz, pack * z_size)
        z_map.append(jnp.pad(block, ((0, 0), (0, width - pack * z_size))))
    z_map = jnp.concatenate(z_map, axis=1)
    order = sorted(range(row_tiles), key=lambda j: (j % 2, j))
    at = jnp.arange(s_size, dtype=jnp.int32)
    far = jnp.array(order, jnp.int32)[at // p_size]
    wanted = ((u ^ far) * column_tiles + (v ^ (at % p_size // p_rows))) * p_rows + at % p_rows
    chosen = (wanted[:, None] == at[None, :]).astype(BF16)
    x_map = dot(chosen, cut(core_x.T, u * TX, TX, 1)).astype(BF16)

    tiles_wide = [count // pack * (width // LANES) for count in counts]
    slabbed, mixed, sums, blocks = {}, {}, {}, {}
    small = []

    def end_y(c, token):
        added = []
        if c == riding:
            added = [one, two]
        group = place[c][0]
        near, *far = after(token, parts[group], *arrived[group])
        near, *send = along_z(near, far, starts[c], counts[c], z_map, slabs, pack, added)
        slabbed[c] = [near] + [to_slab(x, step + 1) for step, x in enumerate(send)]
        return send[0]

    def end_z(c, token):
        tall = TX * tiles_wide[c]
        near, *far = after(token, *slabbed[c])
        keep, send, *rest = along_x(near, far, x_map, tall, [three] if c == riding else [])
        small.extend(rest)
        mixed[c] = (keep, flip(send, column_tiles))
        return send

    def add_near(c, token):
        keep, got = after(token, *mixed[c])
        mine, send = add_split(keep, got, p_size * tiles_wide[c], True)
        sums[c] = (mine, flip(send, 2 * column_tiles))
        return send

    def add_far(c, token):
        mine, got = after(token, *sums[c])
        near, away, *rest = add_split(mine, got, p_size // 2 * tiles_wide[c], False)
        small.extend(rest)
        blocks[c] = (near, away)
        return away

    def exchange(group, sketches):
        near = jnp.concatenate([blocks[c][0].astype(BF16) for c in group], axis=0)
        rows = near.shape[0]
        sent = [blocks[c][1] for c in group]
        if sketches is not None:
            sent.append(sketches.astype(BF16))
        got = flip(jnp.concatenate(sent, axis=0), column_tiles // 2)
        if sketches is not None:
            sketches = sketches + got[rows:].astype(F32)
        pieces = jnp.concatenate([near, got[:rows]], axis=0)
        bit = column_tiles // 4
        while bit:
            size = pieces.shape[0]
            sent = pieces
            if sketches is not None:
                sent = jnp.concatenate([pieces, sketches.astype(BF16)], axis=0)
            got = flip(sent, bit)
            if sketches is not None:
                sketches = sketches + got[size:].astype(F32)
            pieces = jnp.concatenate([pieces, got[:size]], axis=0)
            bit //= 2
        return pieces, sketches

    def sketch_rows():
        slab_cut = lambda x, rows: lax.dynamic_index_in_dim(
            x.reshape(-1, slabs, rows, LANES), slab, 1, False
        ).reshape(-1, LANES)
        mine = slab_cut(small[0][:TX], one_rows)
        theirs = slab_cut(small[1][:TY], two_rows)
        turns = column_tiles // row_tiles
        theirs = jnp.concatenate([jnp.where(v == u * turns + n, theirs, 0.0) for n in range(turns)])
        last = cut(small[1][TY:], u * (k // row_tiles), k // row_tiles, 0)
        return jnp.concatenate([mine, theirs, last], axis=0)

    stages = [end_y, end_z, add_near, add_far]
    begun = [2 * sum(counts[:c]) / UNIT for c in range(chunks)]
    order = sorted((begun[c] + LAG * n, n, c) for c in range(chunks) for n in range(len(stages)))
    token, ends = parts[0], -1
    for at, (_, n, c) in enumerate(order):
        if at == ends:
            token = first
        token = stages[n](c, token)
        if stages[n] is add_far and c == early - 1:
            first, sketches = exchange(range(early), sketch_rows())
            ends = at + WAIT if WAIT else -1
    last, _ = exchange(range(early, chunks), None)
    mode_one, mode_two, mode_three, core_sketch = unpack(
        [first, last],
        [counts[:early], counts[early:]],
        sketches,
        v,
        [(one_rows, k), (two_rows, k), (three_rows, nz), (p_rows, s_size, z_size)],
        (pack, width, column_tiles),
    )
    return mode_one, mode_two, mode_three, core_sketch


def solution(mesh):
    return jax.shard_map(
        shards,
        mesh=mesh,
        in_specs=(
            P("xy", None, None, "gz"),
            P(),
            P(),
            P("gz", None),
            P(),
            P(),
            P(),
            P(),
            P("gz", None),
            P("gz", None),
        ),
        out_specs=(
            P(("xy", "gz"), None),
            P(("xy", "gz"), None),
            P("xy", "gz"),
            P("xy", None, "gz"),
        ),
        check_vma=False,
    )
```

time: 540 us -> 89.1 us (0.16)
  waiting for transfers between devices: 410 us -> 23.4 us
  blocking collectives: 59.7 us -> 0 us
  matrix products: 37.4 us -> 0.22 us
  starting transfers between devices: 0.34 us -> 34.9 us
  Pallas kernels: 0 us -> 23.6 us
  between operations: 14.6 us -> 1.15 us
  local copies, waits for them, and re-layouts: 11.7 us -> 4.67 us
  other arithmetic: 6.47 us -> 0.68 us
    reduce_scatter x3 -> x0, waiting for transfers between devices: 409 us -> none  [the longest x1 197 us: shards(): lax.psum_scatter(jnp.einsum('pbz,bq->pqz', lowered, y_rows, preferred_ele...]
    unnamed x1 -> x0, blocking collectives: 59.7 us -> none
    dot_general x5 -> x1, matrix products: 37.4 us -> 0.22 us  [dot(): return jnp.dot(a, b, preferred_element_type=F32)]
    ppermute x0 -> x29, starting transfers between devices: none -> 34.9 us  [the longest x17 18.8 us: flip(): return lax.ppermute(x, 'xy', [(i, i ^ bit) for i in range(tiles)])]
    pallas_call x0 -> x27, Pallas kernels: none -> 23.6 us  [the longest x1 6.98 us: modes(): pl.pallas_call(modes_kernel, grid_spec=pltpu.PrefetchScalarGridSpec(num_s...]
    ppermute x0 -> x29, waiting for transfers between devices: none -> 23.4 us  [the longest x17 15.4 us: flip(): return lax.ppermute(x, 'xy', [(i, i ^ bit) for i in range(tiles)])]
    unnamed x20 -> x34, local copies, waits for them, and re-layouts: 11.3 us -> 2.75 us
  transfers between devices with their start and end apart: 4 -> 29, of which waited for: 3 -> 13; matrix products, arithmetic and copies ran while one was open for 4% -> 3% of each run, Pallas kernels for 0% -> 17%
where the time goes in v1:
time: 89.1 us; the launch traced here: 88.6 us
  starting transfers between devices  34.9 us (39%)
  Pallas kernels  23.6 us (26%)
  waiting for transfers between devices  23.4 us (26%)
  local copies, waits for them, and re-layouts  4.67 us (5%)
  between operations  1.15 us (1%)
    ppermute x17, starting transfers between devices, flip(): return lax.ppermute(x, 'xy', [(i, i ^ bit) for i in range(tiles)])  18.8 us
    ppermute x17, waiting for transfers between devices, flip(): return lax.ppermute(x, 'xy', [(i, i ^ bit) for i in range(tiles)])  15.4 us
    ppermute x6, starting transfers between devices, to_slab(): lax.ppermute(x, 'gz', [(i, (i + step) % slabs) for i in range(slabs)])  9.29 us
    ppermute x6, waiting for transfers between devices, to_pair(): return lax.ppermute(x, 'xy', [(i, target(i)) for i in range(tiles)])  7.94 us
    pallas_call x1, Pallas kernels, modes(): pl.pallas_call(modes_kernel, grid_spec=pltpu.PrefetchScalarGridSpec(num_s...  6.98 us
    pallas_call x1, Pallas kernels, plane(): pl.pallas_call(functools.partial(plane_kernel, targets), grid_spec=pltpu....  6.89 us
    ppermute x6, starting transfers between devices, to_pair(): return lax.ppermute(x, 'xy', [(i, target(i)) for i in range(tiles)])  6.83 us
    pallas_call x6, Pallas kernels, along_x(): pl.pallas_call(functools.partial(along_x_kernel, tall, len(riders)), out_...  3.97 us
  transfers between devices with their start and end apart: 29, of which 13 were waited for; matrix products, arithmetic and copies ran while one was open for 3% of the time, Pallas kernels for 17%

profile of v1, /device:TPU:0, one launch (start us, length us, event | category | flops | bytes accessed | tf_op | source)
XLA Modules:
  0.0 88.6 jit_solution(6754099974290154897)
XLA Ops:
  0.6 0.5 collective-permute-start
  1.2 0.7 stack.20.tile.place
  1.8 7.0 %modes.1 = (f32[128,128]{1,0:T(8,128)}, f32[128,128]{1,0:T(8,128)}, f32[96,128]{1,0:T(8,128)}) custom-call(s32[5]{0:T(128)} %stack.20.tile.place, bf16[128,128,128]{2,1,0:T(8,128)(2,1)} %bitcast.38, bf16[128,128,128]{2,1,0:T(8,128)(2,1)} %bitcast.39, bf16[96,128]{1,0:T(8,128)(2,1)} %bitcast.59, bf16[96,128]{1,0:T(8,128)(2,1)} %bitcast.60, ...), custom_call_target="tpu_custom_call" | custom-call | flops 1476395008 | bytes 4194304 | tf_op jit(solution)/shard_map/modes/pallas_call | solution.py:74
  8.9 6.9 %plane.1 = (bf16[128,8,128]{2,1,0:T(8,128)(2,1)}, bf16[128,8,128]{2,1,0:T(8,128)(2,1)}, bf16[128,8,128]{2,1,0:T(8,128)(2,1)}, bf16[128,8,128]{2,1,0:T(8,128)(2,1...) custom-call(s32[5]{0:T(128)} %stack.20.tile.place, ...), custom_call_target="tpu_custom_call" | custom-call | flops 805306368 | bytes 12582912 | tf_op jit(solution)/shard_map/plane/pallas_call | solution.py:148
  15.8 2.7 %collective-permute-start.1 = (bf16[128,8,128]{2,1,0:T(8,128)(2,1)}, bf16[128,8,128]{2,1,0:T(8,128)(2,1)S(1)}, u32[]{:S(2)}, u32[]{:S(2)}) collective-permute-start(bf16[128,8,128]{2,1,0:T(8,128)(2,1)} %get-tuple-element.123), channel_id=1, source_target_pairs={{0,4},{2,6},{4,0},{6,2},{8,12},{10,14},{12,8},{14,10},{16,20},{18,... | collective-permute-start | bytes 786440 | tf_op jit(solution)/shard_map/ppermute | solution.py:398
  19.9 1.9 %collective-permute-start.4 = (bf16[128,8,128]{2,1,0:T(8,128)(2,1)S(1)}, bf16[128,8,128]{2,1,0:T(8,128)(2,1)S(1)}, u32[]{:S(2)}, u32[]{:S(2)}) collective-permute-start(bf16[128,8,128]{2,1,0:T(8,128)(2,1)S(1)} %copy-done.14), channel_id=1, source_target_pairs={{0,4},{2,6},{4,0},{6,2},{8,12},{10,14},{12,8},{14,10},{16,20},{18,... | collective-permute-start | bytes 786440 | tf_op jit(solution)/shard_map/ppermute | solution.py:398
  22.0 3.8 %collective-permute-done.1.refs_0_ = bf16[128,8,128]{2,1,0:T(8,128)(2,1)S(1)} collective-permute-done((bf16[128,8,128]{2,1,0:T(8,128)(2,1)}, bf16[128,8,128]{2,1,0:T(8,128)(2,1)S(1)}, u32[]{:S(2)}, u32[]{:S(2)}) %collective-permute-start.1) | collective-permute-done | bytes 262176 | tf_op jit(solution)/shard_map/ppermute | solution.py:398
  26.3 2.1 %collective-permute-start.3 = (bf16[768,128]{1,0:T(8,128)(2,1)S(1)}, bf16[768,128]{1,0:T(8,128)(2,1)S(1)}, u32[]{:S(2)}, u32[]{:S(2)}) collective-permute-start(bf16[768,128]{1,0:T(8,128)(2,1)S(1)} %get-tuple-element.127), channel_id=1, source_target_pairs={{0,1},{1,0},{2,3},{3,2},{4,5},{5,4},{6,7},{7,6},{8,9},{9,8},{10,11... | collective-permute-start | bytes 589832 | tf_op jit(solution)/shard_map/ppermute | solution.py:403
  28.3 3.1 %collective-permute-done.2.refs_0_ = bf16[128,8,128]{2,1,0:T(8,128)(2,1)S(1)} collective-permute-done((bf16[128,8,128]{2,1,0:T(8,128)(2,1)}, bf16[128,8,128]{2,1,0:T(8,128)(2,1)S(1)}, u32[]{:S(2)}, u32[]{:S(2)}) %collective-permute-start.2) | collective-permute-done | bytes 262176 | tf_op jit(solution)/shard_map/ppermute | solution.py:398
  31.9 2.1 %collective-permute-start.5 = (bf16[1024,128]{1,0:T(8,128)(2,1)S(1)}, bf16[1024,128]{1,0:T(8,128)(2,1)S(1)}, u32[]{:S(2)}, u32[]{:S(2)}) collective-permute-start(bf16[1024,128]{1,0:T(8,128)(2,1)S(1)} %get-tuple-element.133), channel_id=1, source_target_pairs={{0,1},{1,0},{2,3},{3,2},{4,5},{5,4},{6,7},{7,6},{8,9},{9,8},{10,11... | collective-permute-start | bytes 786440 | tf_op jit(solution)/shard_map/ppermute | solution.py:403
  34.5 1.6 %collective-permute-start.7 = (bf16[576,128]{1,0:T(8,128)(2,1)S(1)}, bf16[576,128]{1,0:T(8,128)(2,1)S(1)}, u32[]{:S(2)}, u32[]{:S(2)}) collective-permute-start(bf16[576,128]{1,0:T(8,128)(2,1)S(1)} %get-tuple-element.138), channel_id=1, source_target_pairs={{0,8},{2,10},{4,12},{6,14},{8,0},{10,2},{12,4},{14,6},{16,24},{18,... | collective-permute-start | bytes 442376 | tf_op jit(solution)/shard_map/ppermute | solution.py:391
  36.1 1.0 %collective-permute-done.4.refs_0_ = bf16[128,8,128]{2,1,0:T(8,128)(2,1)S(1)} collective-permute-done((bf16[128,8,128]{2,1,0:T(8,128)(2,1)S(1)}, bf16[128,8,128]{2,1,0:T(8,128)(2,1)S(1)}, u32[]{:S(2)}, u32[]{:S(2)}) %collective-permute-start.4) | collective-permute-done | bytes 262176 | tf_op jit(solution)/shard_map/ppermute | solution.py:398
  37.1 1.1 %along_z.8 = (f32[768,128]{1,0:T(8,128)S(1)}, bf16[768,128]{1,0:T(8,128)(2,1)}) custom-call(bf16[128,8,128]{2,1,0:T(8,128)(2,1)S(1)} %copy-done.4, bf16[128,8,128]{2,1,0:T(8,128)(2,1)S(1)} %collective-permute-done.4.refs_0_, bf16[512,768]{1,0:T(8,128)(2,1)S(1)} %pad_maximum_fusion.refs_1_), custom_call_target="tpu_custom_call" | custom-call | flops 201326592 | bytes 1048576 | tf_op jit(solution)/shard_map/along_z/pallas_call | solution.py:204
  38.2 2.0 %collective-permute-start.8 = (bf16[768,128]{1,0:T(8,128)(2,1)}, bf16[768,128]{1,0:T(8,128)(2,1)}, u32[]{:S(2)}, u32[]{:S(2)}) collective-permute-start(bf16[768,128]{1,0:T(8,128)(2,1)} %get-tuple-element.143), channel_id=1, source_target_pairs={{0,1},{1,0},{2,3},{3,2},{4,5},{5,4},{6,7},{7,6},{8,9},{9,8},{10,11... | collective-permute-start | bytes 589832 | tf_op jit(solution)/shard_map/ppermute | solution.py:403
  40.2 1.5 %collective-permute-start.9 = (bf16[128,8,128]{2,1,0:T(8,128)(2,1)}, bf16[128,8,128]{2,1,0:T(8,128)(2,1)S(1)}, u32[]{:S(2)}, u32[]{:S(2)}) collective-permute-start(bf16[128,8,128]{2,1,0:T(8,128)(2,1)} %get-tuple-element.164), channel_id=1, source_target_pairs={{0,4},{2,6},{4,0},{6,2},{8,12},{10,14},{12,8},{14,10},{16,20},{18,... | collective-permute-start | bytes 786440 | tf_op jit(solution)/shard_map/ppermute | solution.py:398
  41.7 0.5 collective-permute-start.13
  42.2 0.9 %along_x.7 = (f32[800,128]{1,0:T(8,128)S(1)}, bf16[800,128]{1,0:T(8,128)(2,1)}, f32[128,128]{1,0:T(8,128)S(1)}) custom-call(f32[1024,128]{1,0:T(8,128)S(1)} %get-tuple-element.145.near, bf16[1024,128]{1,0:T(8,128)(2,1)S(1)} %collective-permute-done.5.refs_0_, bf16[192,128]{1,0:T(8,128)(2,1)S(1)} %convolution_convert_fusion.refs_1_, f32[96,128]{1,0:T(8,128)S(1)} %copy-done.11), custom_call_target="tpu_custom_call" | custom-call | flops 37748736 | bytes 589824 | tf_op jit(solution)/shard_map/along_x/pallas_call | solution.py:253
  43.1 0.6 copy-done.12
  43.7 1.6 %collective-permute-start.10 = (bf16[800,128]{1,0:T(8,128)(2,1)}, bf16[800,128]{1,0:T(8,128)(2,1)S(1)}, u32[]{:S(2)}, u32[]{:S(2)}) collective-permute-start(bf16[800,128]{1,0:T(8,128)(2,1)} %get-tuple-element.149), channel_id=1, source_target_pairs={{0,8},{2,10},{4,12},{6,14},{8,0},{10,2},{12,4},{14,6},{16,24},{18,... | collective-permute-start | bytes 614408 | tf_op jit(solution)/shard_map/ppermute | solution.py:391
  45.3 1.1 %along_z.9 = (f32[768,128]{1,0:T(8,128)S(1)}, bf16[768,128]{1,0:T(8,128)(2,1)}) custom-call(bf16[128,8,128]{2,1,0:T(8,128)(2,1)S(1)} %copy-done.3, bf16[128,8,128]{2,1,0:T(8,128)(2,1)S(1)} %collective-permute-done.6.refs_0_, bf16[512,768]{1,0:T(8,128)(2,1)S(1)} %pad_maximum_fusion.refs_1_), custom_call_target="tpu_custom_call" | custom-call | flops 201326592 | bytes 1048576 | tf_op jit(solution)/shard_map/along_z/pallas_call | solution.py:204
  46.4 0.7 copy-done.7
  47.1 1.0 %collective-permute-start.11 = (bf16[768,128]{1,0:T(8,128)(2,1)}, bf16[768,128]{1,0:T(8,128)(2,1)}, u32[]{:S(2)}, u32[]{:S(2)}) collective-permute-start(bf16[768,128]{1,0:T(8,128)(2,1)} %get-tuple-element.154), channel_id=1, source_target_pairs={{0,1},{1,0},{2,3},{3,2},{4,5},{5,4},{6,7},{7,6},{8,9},{9,8},{10,11... | collective-permute-start | bytes 589832 | tf_op jit(solution)/shard_map/ppermute | solution.py:403
  48.1 0.9 %copy-done.8 = bf16[576,128]{1,0:T(8,128)(2,1)S(1)} copy-done((bf16[576,128]{1,0:T(8,128)(2,1)S(1)}, bf16[576,128]{1,0:T(8,128)(2,1)}, u32[]{:S(2)}) %copy-start.8) | copy-done | bytes 147480
  49.0 2.7 %collective-permute-start.12 = (bf16[288,128]{1,0:T(8,128)(2,1)S(1)}, bf16[288,128]{1,0:T(8,128)(2,1)S(1)}, u32[]{:S(2)}, u32[]{:S(2)}) collective-permute-start(bf16[288,128]{1,0:T(8,128)(2,1)S(1)} %get-tuple-element.158), channel_id=1, source_target_pairs={{0,16},{2,18},{4,20},{6,22},{8,24},{10,26},{12,28},{14,30},{16,0},... | collective-permute-start | bytes 221192 | tf_op jit(solution)/shard_map/ppermute | solution.py:391
  51.7 0.8 constant_dynamic-slice_fusion.1
  52.4 1.2 %along_x.8 = (f32[576,128]{1,0:T(8,128)S(1)}, bf16[576,128]{1,0:T(8,128)(2,1)S(1)}) custom-call(f32[768,128]{1,0:T(8,128)S(1)} %get-tuple-element.160.near, bf16[768,128]{1,0:T(8,128)(2,1)} %collective-permute-done.8.refs_0_, bf16[192,128]{1,0:T(8,128)(2,1)S(1)} %convolution_convert_fusion.refs_1_), custom_call_target="tpu_custom_call" | custom-call | flops 37748736 | bytes 589824 | tf_op jit(solution)/shard_map/along_x/pallas_call | solution.py:253
  53.6 0.5 collective-permute-start.14
  54.6 1.1 %collective-permute-start.15 = (bf16[768,128]{1,0:T(8,128)(2,1)S(1)}, bf16[768,128]{1,0:T(8,128)(2,1)S(1)}, u32[]{:S(2)}, u32[]{:S(2)}) collective-permute-start(bf16[768,128]{1,0:T(8,128)(2,1)S(1)} %get-tuple-element.167), channel_id=1, source_target_pairs={{0,1},{1,0},{2,3},{3,2},{4,5},{5,4},{6,7},{7,6},{8,9},{9,8},{10,11... | collective-permute-start | bytes 589832 | tf_op jit(solution)/shard_map/ppermute | solution.py:403
  56.2 1.2 %along_x.9 = (f32[576,128]{1,0:T(8,128)S(1)}, bf16[576,128]{1,0:T(8,128)(2,1)S(1)}) custom-call(f32[768,128]{1,0:T(8,128)S(1)} %get-tuple-element.173.near, bf16[768,128]{1,0:T(8,128)(2,1)} %collective-permute-done.11.refs_0_, bf16[192,128]{1,0:T(8,128)(2,1)S(1)} %convolution_convert_fusion.refs_1_), custom_call_target="tpu_custom_call" | custom-call | flops 37748736 | bytes 589824 | tf_op jit(solution)/shard_map/along_x/pallas_call | solution.py:253
  57.4 1.6 %collective-permute-start.17 = (bf16[576,128]{1,0:T(8,128)(2,1)S(1)}, bf16[576,128]{1,0:T(8,128)(2,1)S(1)}, u32[]{:S(2)}, u32[]{:S(2)}) collective-permute-start(bf16[576,128]{1,0:T(8,128)(2,1)S(1)} %get-tuple-element.175), channel_id=1, source_target_pairs={{0,8},{2,10},{4,12},{6,14},{8,0},{10,2},{12,4},{14,6},{16,24},{18,... | collective-permute-start | bytes 442376 | tf_op jit(solution)/shard_map/ppermute | solution.py:391
  59.4 1.0 %collective-permute-start.18 = (bf16[768,128]{1,0:T(8,128)(2,1)S(1)}, bf16[768,128]{1,0:T(8,128)(2,1)S(1)}, u32[]{:S(2)}, u32[]{:S(2)}) collective-permute-start(bf16[768,128]{1,0:T(8,128)(2,1)S(1)} %get-tuple-element.184), channel_id=1, source_target_pairs={{0,1},{1,0},{2,3},{3,2},{4,5},{5,4},{6,7},{7,6},{8,9},{9,8},{10,11... | collective-permute-start | bytes 589832 | tf_op jit(solution)/shard_map/ppermute | solution.py:403
  60.5 2.0 %collective-permute-done.14.far = bf16[576,128]{1,0:T(8,128)(2,1)S(1)} collective-permute-done((bf16[576,128]{1,0:T(8,128)(2,1)S(1)}, bf16[576,128]{1,0:T(8,128)(2,1)S(1)}, u32[]{:S(2)}, u32[]{:S(2)}) %collective-permute-start.14) | collective-permute-done | bytes 147488 | tf_op jit(solution)/shard_map/ppermute | solution.py:391
  62.5 0.7 collective-permute-start.19
  63.4 0.5 collective-permute-start.22
  64.0 0.5 collective-permute-done.16.far
  64.6 1.8 %collective-permute-done.17.far = bf16[576,128]{1,0:T(8,128)(2,1)S(1)} collective-permute-done((bf16[576,128]{1,0:T(8,128)(2,1)S(1)}, bf16[576,128]{1,0:T(8,128)(2,1)S(1)}, u32[]{:S(2)}, u32[]{:S(2)}) %collective-permute-start.17) | collective-permute-done | bytes 147488 | tf_op jit(solution)/shard_map/ppermute | solution.py:391
  66.3 1.7 %collective-permute-start.23 = (bf16[288,128]{1,0:T(8,128)(2,1)S(1)}, bf16[288,128]{1,0:T(8,128)(2,1)S(1)}, u32[]{:S(2)}, u32[]{:S(2)}) collective-permute-start(bf16[288,128]{1,0:T(8,128)(2,1)S(1)} %get-tuple-element.201), channel_id=1, source_target_pairs={{0,16},{2,18},{4,20},{6,22},{8,24},{10,26},{12,28},{14,30},{16,0},... | collective-permute-start | bytes 221192 | tf_op jit(solution)/shard_map/ppermute | solution.py:391
  68.3 1.8 %collective-permute-start.24 = (bf16[576,128]{1,0:T(8,128)(2,1)S(1)}, bf16[576,128]{1,0:T(8,128)(2,1)S(1)}, u32[]{:S(2)}, u32[]{:S(2)}) collective-permute-start(bf16[576,128]{1,0:T(8,128)(2,1)S(1)} %get-tuple-element.205), channel_id=1, source_target_pairs={{0,8},{2,10},{4,12},{6,14},{8,0},{10,2},{12,4},{14,6},{16,24},{18,... | collective-permute-start | bytes 442376 | tf_op jit(solution)/shard_map/ppermute | solution.py:391
  70.1 1.6 %collective-permute-start.20 = (bf16[584,128]{1,0:T(8,128)(2,1)S(1)}, bf16[584,128]{1,0:T(8,128)(2,1)S(1)}, u32[]{:S(2)}, u32[]{:S(2)}) collective-permute-start(bf16[584,128]{1,0:T(8,128)(2,1)S(1)} %pad_maximum_fusion.2), channel_id=1, source_target_pairs={{0,4},{2,6},{4,0},{6,2},{8,12},{10,14},{12,8},{14,10},{16,20},{18,... | collective-permute-start | bytes 448520 | tf_op jit(solution)/shard_map/ppermute | solution.py:391
  72.1 0.7 collective-permute-start.25
  72.8 1.3 %collective-permute-done.23.far = bf16[288,128]{1,0:T(8,128)(2,1)S(1)} collective-permute-done((bf16[288,128]{1,0:T(8,128)(2,1)S(1)}, bf16[288,128]{1,0:T(8,128)(2,1)S(1)}, u32[]{:S(2)}, u32[]{:S(2)}) %collective-permute-start.23) | collective-permute-done | bytes 73760 | tf_op jit(solution)/shard_map/ppermute | solution.py:391
  74.4 1.2 %collective-permute-start.26 = (bf16[288,128]{1,0:T(8,128)(2,1)S(1)}, bf16[288,128]{1,0:T(8,128)(2,1)S(1)}, u32[]{:S(2)}, u32[]{:S(2)}) collective-permute-start(bf16[288,128]{1,0:T(8,128)(2,1)S(1)} %get-tuple-element.225), channel_id=1, source_target_pairs={{0,16},{2,18},{4,20},{6,22},{8,24},{10,26},{12,28},{14,30},{16,0},... | collective-permute-start | bytes 221192 | tf_op jit(solution)/shard_map/ppermute | solution.py:391
  75.6 2.7 %collective-permute-done.25.far = bf16[288,128]{1,0:T(8,128)(2,1)S(1)} collective-permute-done((bf16[288,128]{1,0:T(8,128)(2,1)S(1)}, bf16[288,128]{1,0:T(8,128)(2,1)S(1)}, u32[]{:S(2)}, u32[]{:S(2)}) %collective-permute-start.25) | collective-permute-done | bytes 73760 | tf_op jit(solution)/shard_map/ppermute | solution.py:391
  78.5 2.0 %collective-permute-done.26.far = bf16[288,128]{1,0:T(8,128)(2,1)S(1)} collective-permute-done((bf16[288,128]{1,0:T(8,128)(2,1)S(1)}, bf16[288,128]{1,0:T(8,128)(2,1)S(1)}, u32[]{:S(2)}, u32[]{:S(2)}) %collective-permute-start.26) | collective-permute-done | bytes 73760 | tf_op jit(solution)/shard_map/ppermute | solution.py:391
  80.6 1.6 %collective-permute-start.27 = (bf16[432,128]{1,0:T(8,128)(2,1)S(1)}, bf16[432,128]{1,0:T(8,128)(2,1)S(1)}, u32[]{:S(2)}, u32[]{:S(2)}) collective-permute-start(bf16[432,128]{1,0:T(8,128)(2,1)S(1)} %pad_maximum_fusion.3), channel_id=1, source_target_pairs={{0,4},{2,6},{4,0},{6,2},{8,12},{10,14},{12,8},{14,10},{16,20},{18,... | collective-permute-start | bytes 331784 | tf_op jit(solution)/shard_map/ppermute | solution.py:391
  82.2 3.2 %collective-permute-done.27 = bf16[432,128]{1,0:T(8,128)(2,1)S(1)} collective-permute-done((bf16[432,128]{1,0:T(8,128)(2,1)S(1)}, bf16[432,128]{1,0:T(8,128)(2,1)S(1)}, u32[]{:S(2)}, u32[]{:S(2)}) %collective-permute-start.27) | collective-permute-done | bytes 110624 | tf_op jit(solution)/shard_map/ppermute | solution.py:391
  85.6 1.4 %collective-permute-done.28 = bf16[864,128]{1,0:T(8,128)(2,1)S(1)} collective-permute-done((bf16[864,128]{1,0:T(8,128)(2,1)S(1)}, bf16[864,128]{1,0:T(8,128)(2,1)S(1)}, u32[]{:S(2)}, u32[]{:S(2)}) %collective-permute-start.28) | collective-permute-done | bytes 221216 | tf_op jit(solution)/shard_map/ppermute | solution.py:391
  87.0 1.6 %unpack.1 = (f32[16,96]{1,0:T(8,128)}, f32[16,96]{1,0:T(8,128)}, f32[6,128]{1,0:T(8,128)}, f32[12,192,96]{2,1,0:T(8,128)}) custom-call(s32[1]{0:T(128)} %bitcast.column, f32[152,128]{1,0:T(8,128)S(1)} %convert_add_fusion.sketches, bf16[1728,128]{1,0:T(8,128)(2,1)S(1)} %slice_dynamic-update-slice_fusion.refs_0_, ...), custom_call_target="tpu_custom_call" | custom-call | flops 884736 | bytes 1769472 | tf_op jit(solution)/shard_map/unpack/pallas_call | solution.py:332
  (100 shorter events, 6.0 us)
Async XLA Ops:
  0.6 33.3 %copy-start = (bf16[512,192]{0,1:T(8,128)(2,1)S(1)}, bf16[512,192]{0,1:T(8,128)(2,1)}, u32[]{:S(2)}) copy-start(bf16[512,192]{0,1:T(8,128)(2,1)} %param.12) | copy-start | bytes 589828
  0.6 8.2 %collective-permute-start = (bf16[128,128,128]{2,1,0:T(8,128)(2,1)}, bf16[128,128,128]{2,1,0:T(8,128)(2,1)}, u32[]{:S(2)}, u32[]{:S(2)}) collective-permute-start(bf16[128,128,128]{2,1,0:T(8,128)(2,1)} %bitcast.37), channel_id=1, source_target_pairs={{0,2},{2,0},{4,6},{6,4},{8,10},{10,8},{12,14},{14,12},{16,18},{18,... | collective-permute-start | bytes 12582920 | tf_op jit(solution)/shard_map/ppermute | solution.py:391
  8.9 9.7 %copy-start.13 = (bf16[128,192]{0,1:T(8,128)(2,1)S(1)}, bf16[128,192]{0,1:T(8,128)(2,1)}, u32[]{:S(2)}) copy-start(bf16[128,192]{0,1:T(8,128)(2,1)} %param.14) | copy-start | bytes 147460
  15.8 10.0 %collective-permute-start.1 = (bf16[128,8,128]{2,1,0:T(8,128)(2,1)}, bf16[128,8,128]{2,1,0:T(8,128)(2,1)S(1)}, u32[]{:S(2)}, u32[]{:S(2)}) collective-permute-start(bf16[128,8,128]{2,1,0:T(8,128)(2,1)} %get-tuple-element.123), channel_id=1, source_target_pairs={{0,4},{2,6},{4,0},{6,2},{8,12},{10,14},{12,8},{14,10},{16,20},{18,... | collective-permute-start | bytes 786440 | tf_op jit(solution)/shard_map/ppermute | solution.py:398
  18.5 13.0 %collective-permute-start.2 = (bf16[128,8,128]{2,1,0:T(8,128)(2,1)}, bf16[128,8,128]{2,1,0:T(8,128)(2,1)S(1)}, u32[]{:S(2)}, u32[]{:S(2)}) collective-permute-start(bf16[128,8,128]{2,1,0:T(8,128)(2,1)} %get-tuple-element.129), channel_id=1, source_target_pairs={{0,4},{2,6},{4,0},{6,2},{8,12},{10,14},{12,8},{14,10},{16,20},{18,... | collective-permute-start | bytes 786440 | tf_op jit(solution)/shard_map/ppermute | solution.py:398
  18.9 1.0 %copy-start.14 = (bf16[128,8,128]{2,1,0:T(8,128)(2,1)S(1)}, bf16[128,8,128]{2,1,0:T(8,128)(2,1)}, u32[]{:S(2)}) copy-start(bf16[128,8,128]{2,1,0:T(8,128)(2,1)} %get-tuple-element.140) | copy-start | bytes 786436
  19.2 6.6 %copy-start.5 = (bf16[128,8,128]{2,1,0:T(8,128)(2,1)S(1)}, bf16[128,8,128]{2,1,0:T(8,128)(2,1)}, u32[]{:S(2)}) copy-start(bf16[128,8,128]{2,1,0:T(8,128)(2,1)} %get-tuple-element.124.near) | copy-start | bytes 786436
  19.5 11.9 %copy-start.6 = (bf16[128,8,128]{2,1,0:T(8,128)(2,1)S(1)}, bf16[128,8,128]{2,1,0:T(8,128)(2,1)}, u32[]{:S(2)}) copy-start(bf16[128,8,128]{2,1,0:T(8,128)(2,1)} %get-tuple-element.130.near) | copy-start | bytes 786436
  19.5 11.9 %copy-start.9 = (f32[128,128]{1,0:T(8,128)S(1)}, f32[128,128]{1,0:T(8,128)}, u32[]{:S(2)}) copy-start(f32[128,128]{1,0:T(8,128)} %get-tuple-element.120.refs_2_) | copy-start | bytes 196612
  19.6 11.9 %copy-start.10 = (f32[128,128]{1,0:T(8,128)S(1)}, f32[128,128]{1,0:T(8,128)}, u32[]{:S(2)}) copy-start(f32[128,128]{1,0:T(8,128)} %get-tuple-element.132.refs_3_) | copy-start | bytes 196612
  19.9 17.2 %collective-permute-start.4 = (bf16[128,8,128]{2,1,0:T(8,128)(2,1)S(1)}, bf16[128,8,128]{2,1,0:T(8,128)(2,1)S(1)}, u32[]{:S(2)}, u32[]{:S(2)}) collective-permute-start(bf16[128,8,128]{2,1,0:T(8,128)(2,1)S(1)} %copy-done.14), channel_id=1, source_target_pairs={{0,4},{2,6},{4,0},{6,2},{8,12},{10,14},{12,8},{14,10},{16,20},{18,... | collective-permute-start | bytes 786440 | tf_op jit(solution)/shard_map/ppermute | solution.py:398
  21.8 21.9 %collective-permute-start.6 = (bf16[128,8,128]{2,1,0:T(8,128)(2,1)}, bf16[128,8,128]{2,1,0:T(8,128)(2,1)S(1)}, u32[]{:S(2)}, u32[]{:S(2)}) collective-permute-start(bf16[128,8,128]{2,1,0:T(8,128)(2,1)} %get-tuple-element.151), channel_id=1, source_target_pairs={{0,4},{2,6},{4,0},{6,2},{8,12},{10,14},{12,8},{14,10},{16,20},{18,... | collective-permute-start | bytes 786440 | tf_op jit(solution)/shard_map/ppermute | solution.py:398
  22.0 15.1 %copy-start.4 = (bf16[128,8,128]{2,1,0:T(8,128)(2,1)S(1)}, bf16[128,8,128]{2,1,0:T(8,128)(2,1)}, u32[]{:S(2)}) copy-start(bf16[128,8,128]{2,1,0:T(8,128)(2,1)} %get-tuple-element.141.near) | copy-start | bytes 786436
  26.3 8.0 %collective-permute-start.3 = (bf16[768,128]{1,0:T(8,128)(2,1)S(1)}, bf16[768,128]{1,0:T(8,128)(2,1)S(1)}, u32[]{:S(2)}, u32[]{:S(2)}) collective-permute-start(bf16[768,128]{1,0:T(8,128)(2,1)S(1)} %get-tuple-element.127), channel_id=1, source_target_pairs={{0,1},{1,0},{2,3},{3,2},{4,5},{5,4},{6,7},{7,6},{8,9},{9,8},{10,11... | collective-permute-start | bytes 589832 | tf_op jit(solution)/shard_map/ppermute | solution.py:403
  31.5 10.7 %copy-start.11 = (f32[96,128]{1,0:T(8,128)S(1)}, f32[96,128]{1,0:T(8,128)}, u32[]{:S(2)}) copy-start(f32[96,128]{1,0:T(8,128)} %get-tuple-element.147.refs_2_) | copy-start | bytes 147460
  31.9 13.4 %copy-start.3 = (bf16[128,8,128]{2,1,0:T(8,128)(2,1)S(1)}, bf16[128,8,128]{2,1,0:T(8,128)(2,1)}, u32[]{:S(2)}) copy-start(bf16[128,8,128]{2,1,0:T(8,128)(2,1)} %get-tuple-element.152.near) | copy-start | bytes 786436
  31.9 9.8 %collective-permute-start.5 = (bf16[1024,128]{1,0:T(8,128)(2,1)S(1)}, bf16[1024,128]{1,0:T(8,128)(2,1)S(1)}, u32[]{:S(2)}, u32[]{:S(2)}) collective-permute-start(bf16[1024,128]{1,0:T(8,128)(2,1)S(1)} %get-tuple-element.133), channel_id=1, source_target_pairs={{0,1},{1,0},{2,3},{3,2},{4,5},{5,4},{6,7},{7,6},{8,9},{9,8},{10,11... | collective-permute-start | bytes 786440 | tf_op jit(solution)/shard_map/ppermute | solution.py:403
  34.5 12.0 %collective-permute-start.7 = (bf16[576,128]{1,0:T(8,128)(2,1)S(1)}, bf16[576,128]{1,0:T(8,128)(2,1)S(1)}, u32[]{:S(2)}, u32[]{:S(2)}) collective-permute-start(bf16[576,128]{1,0:T(8,128)(2,1)S(1)} %get-tuple-element.138), channel_id=1, source_target_pairs={{0,8},{2,10},{4,12},{6,14},{8,0},{10,2},{12,4},{14,6},{16,24},{18,... | collective-permute-start | bytes 442376 | tf_op jit(solution)/shard_map/ppermute | solution.py:391
  38.2 10.8 %collective-permute-start.8 = (bf16[768,128]{1,0:T(8,128)(2,1)}, bf16[768,128]{1,0:T(8,128)(2,1)}, u32[]{:S(2)}, u32[]{:S(2)}) collective-permute-start(bf16[768,128]{1,0:T(8,128)(2,1)} %get-tuple-element.143), channel_id=1, source_target_pairs={{0,1},{1,0},{2,3},{3,2},{4,5},{5,4},{6,7},{7,6},{8,9},{9,8},{10,11... | collective-permute-start | bytes 589832 | tf_op jit(solution)/shard_map/ppermute | solution.py:403
  40.2 13.5 %collective-permute-start.9 = (bf16[128,8,128]{2,1,0:T(8,128)(2,1)}, bf16[128,8,128]{2,1,0:T(8,128)(2,1)S(1)}, u32[]{:S(2)}, u32[]{:S(2)}) collective-permute-start(bf16[128,8,128]{2,1,0:T(8,128)(2,1)} %get-tuple-element.164), channel_id=1, source_target_pairs={{0,4},{2,6},{4,0},{6,2},{8,12},{10,14},{12,8},{14,10},{16,20},{18,... | collective-permute-start | bytes 786440 | tf_op jit(solution)/shard_map/ppermute | solution.py:398
  41.7 17.3 %collective-permute-start.13 = (bf16[128,8,128]{2,1,0:T(8,128)(2,1)}, bf16[128,8,128]{2,1,0:T(8,128)(2,1)S(1)}, u32[]{:S(2)}, u32[]{:S(2)}) collective-permute-start(bf16[128,8,128]{2,1,0:T(8,128)(2,1)} %get-tuple-element.181), channel_id=1, source_target_pairs={{0,4},{2,6},{4,0},{6,2},{8,12},{10,14},{12,8},{14,10},{16,20},{18,... | collective-permute-start | bytes 786440 | tf_op jit(solution)/shard_map/ppermute | solution.py:398
  42.2 11.9 %copy-start.2 = (bf16[128,8,128]{2,1,0:T(8,128)(2,1)S(1)}, bf16[128,8,128]{2,1,0:T(8,128)(2,1)}, u32[]{:S(2)}) copy-start(bf16[128,8,128]{2,1,0:T(8,128)(2,1)} %get-tuple-element.165.near) | copy-start | bytes 786436
  43.1 0.6 copy-start.12
  43.7 10.9 %collective-permute-start.10 = (bf16[800,128]{1,0:T(8,128)(2,1)}, bf16[800,128]{1,0:T(8,128)(2,1)S(1)}, u32[]{:S(2)}, u32[]{:S(2)}) collective-permute-start(bf16[800,128]{1,0:T(8,128)(2,1)} %get-tuple-element.149), channel_id=1, source_target_pairs={{0,8},{2,10},{4,12},{6,14},{8,0},{10,2},{12,4},{14,6},{16,24},{18,... | collective-permute-start | bytes 614408 | tf_op jit(solution)/shard_map/ppermute | solution.py:391
  46.4 0.7 copy-start.7
  47.1 8.7 %collective-permute-start.11 = (bf16[768,128]{1,0:T(8,128)(2,1)}, bf16[768,128]{1,0:T(8,128)(2,1)}, u32[]{:S(2)}, u32[]{:S(2)}) collective-permute-start(bf16[768,128]{1,0:T(8,128)(2,1)} %get-tuple-element.154), channel_id=1, source_target_pairs={{0,1},{1,0},{2,3},{3,2},{4,5},{5,4},{6,7},{7,6},{8,9},{9,8},{10,11... | collective-permute-start | bytes 589832 | tf_op jit(solution)/shard_map/ppermute | solution.py:403
  48.1 0.9 %copy-start.8 = (bf16[576,128]{1,0:T(8,128)(2,1)S(1)}, bf16[576,128]{1,0:T(8,128)(2,1)}, u32[]{:S(2)}) copy-start(bf16[576,128]{1,0:T(8,128)(2,1)} %copy-done.7) | copy-start | bytes 442372
  49.0 8.3 %collective-permute-start.12 = (bf16[288,128]{1,0:T(8,128)(2,1)S(1)}, bf16[288,128]{1,0:T(8,128)(2,1)S(1)}, u32[]{:S(2)}, u32[]{:S(2)}) collective-permute-start(bf16[288,128]{1,0:T(8,128)(2,1)S(1)} %get-tuple-element.158), channel_id=1, source_target_pairs={{0,16},{2,18},{4,20},{6,22},{8,24},{10,26},{12,28},{14,30},{16,0},... | collective-permute-start | bytes 221192 | tf_op jit(solution)/shard_map/ppermute | solution.py:391
  52.4 6.6 %copy-start.1 = (bf16[128,8,128]{2,1,0:T(8,128)(2,1)S(1)}, bf16[128,8,128]{2,1,0:T(8,128)(2,1)}, u32[]{:S(2)}) copy-start(bf16[128,8,128]{2,1,0:T(8,128)(2,1)} %get-tuple-element.182.near) | copy-start | bytes 786436
  53.6 8.8 %collective-permute-start.14 = (bf16[576,128]{1,0:T(8,128)(2,1)S(1)}, bf16[576,128]{1,0:T(8,128)(2,1)S(1)}, u32[]{:S(2)}, u32[]{:S(2)}) collective-permute-start(bf16[576,128]{1,0:T(8,128)(2,1)S(1)} %get-tuple-element.162), channel_id=1, source_target_pairs={{0,8},{2,10},{4,12},{6,14},{8,0},{10,2},{12,4},{14,6},{16,24},{18,... | collective-permute-start | bytes 442376 | tf_op jit(solution)/shard_map/ppermute | solution.py:391
  54.6 8.6 %collective-permute-start.15 = (bf16[768,128]{1,0:T(8,128)(2,1)S(1)}, bf16[768,128]{1,0:T(8,128)(2,1)S(1)}, u32[]{:S(2)}, u32[]{:S(2)}) collective-permute-start(bf16[768,128]{1,0:T(8,128)(2,1)S(1)} %get-tuple-element.167), channel_id=1, source_target_pairs={{0,1},{1,0},{2,3},{3,2},{4,5},{5,4},{6,7},{7,6},{8,9},{9,8},{10,11... | collective-permute-start | bytes 589832 | tf_op jit(solution)/shard_map/ppermute | solution.py:403
  55.8 8.6 %collective-permute-start.16 = (bf16[512,128]{1,0:T(8,128)(2,1)S(1)}, bf16[512,128]{1,0:T(8,128)(2,1)S(1)}, u32[]{:S(2)}, u32[]{:S(2)}) collective-permute-start(bf16[512,128]{1,0:T(8,128)(2,1)S(1)} %get-tuple-element.171), channel_id=1, source_target_pairs={{0,16},{2,18},{4,20},{6,22},{8,24},{10,26},{12,28},{14,30},{16,0},... | collective-permute-start | bytes 393224 | tf_op jit(solution)/shard_map/ppermute | solution.py:391
  57.4 8.9 %collective-permute-start.17 = (bf16[576,128]{1,0:T(8,128)(2,1)S(1)}, bf16[576,128]{1,0:T(8,128)(2,1)S(1)}, u32[]{:S(2)}, u32[]{:S(2)}) collective-permute-start(bf16[576,128]{1,0:T(8,128)(2,1)S(1)} %get-tuple-element.175), channel_id=1, source_target_pairs={{0,8},{2,10},{4,12},{6,14},{8,0},{10,2},{12,4},{14,6},{16,24},{18,... | collective-permute-start | bytes 442376 | tf_op jit(solution)/shard_map/ppermute | solution.py:391
  59.4 8.6 %collective-permute-start.18 = (bf16[768,128]{1,0:T(8,128)(2,1)S(1)}, bf16[768,128]{1,0:T(8,128)(2,1)S(1)}, u32[]{:S(2)}, u32[]{:S(2)}) collective-permute-start(bf16[768,128]{1,0:T(8,128)(2,1)S(1)} %get-tuple-element.184), channel_id=1, source_target_pairs={{0,1},{1,0},{2,3},{3,2},{4,5},{5,4},{6,7},{7,6},{8,9},{9,8},{10,11... | collective-permute-start | bytes 589832 | tf_op jit(solution)/shard_map/ppermute | solution.py:403
  62.5 7.6 %collective-permute-start.19 = (bf16[288,128]{1,0:T(8,128)(2,1)S(1)}, bf16[288,128]{1,0:T(8,128)(2,1)S(1)}, u32[]{:S(2)}, u32[]{:S(2)}) collective-permute-start(bf16[288,128]{1,0:T(8,128)(2,1)S(1)} %get-tuple-element.188), channel_id=1, source_target_pairs={{0,16},{2,18},{4,20},{6,22},{8,24},{10,26},{12,28},{14,30},{16,0},... | collective-permute-start | bytes 221192 | tf_op jit(solution)/shard_map/ppermute | solution.py:391
  63.4 8.6 %collective-permute-start.22 = (bf16[576,128]{1,0:T(8,128)(2,1)S(1)}, bf16[576,128]{1,0:T(8,128)(2,1)S(1)}, u32[]{:S(2)}, u32[]{:S(2)}) collective-permute-start(bf16[576,128]{1,0:T(8,128)(2,1)S(1)} %get-tuple-element.192), channel_id=1, source_target_pairs={{0,8},{2,10},{4,12},{6,14},{8,0},{10,2},{12,4},{14,6},{16,24},{18,... | collective-permute-start | bytes 442376 | tf_op jit(solution)/shard_map/ppermute | solution.py:391
  66.3 7.8 %collective-permute-start.23 = (bf16[288,128]{1,0:T(8,128)(2,1)S(1)}, bf16[288,128]{1,0:T(8,128)(2,1)S(1)}, u32[]{:S(2)}, u32[]{:S(2)}) collective-permute-start(bf16[288,128]{1,0:T(8,128)(2,1)S(1)} %get-tuple-element.201), channel_id=1, source_target_pairs={{0,16},{2,18},{4,20},{6,22},{8,24},{10,26},{12,28},{14,30},{16,0},... | collective-permute-start | bytes 221192 | tf_op jit(solution)/shard_map/ppermute | solution.py:391
  68.3 6.1 %collective-permute-start.24 = (bf16[576,128]{1,0:T(8,128)(2,1)S(1)}, bf16[576,128]{1,0:T(8,128)(2,1)S(1)}, u32[]{:S(2)}, u32[]{:S(2)}) collective-permute-start(bf16[576,128]{1,0:T(8,128)(2,1)S(1)} %get-tuple-element.205), channel_id=1, source_target_pairs={{0,8},{2,10},{4,12},{6,14},{8,0},{10,2},{12,4},{14,6},{16,24},{18,... | collective-permute-start | bytes 442376 | tf_op jit(solution)/shard_map/ppermute | solution.py:391
  70.1 8.3 %collective-permute-start.20 = (bf16[584,128]{1,0:T(8,128)(2,1)S(1)}, bf16[584,128]{1,0:T(8,128)(2,1)S(1)}, u32[]{:S(2)}, u32[]{:S(2)}) collective-permute-start(bf16[584,128]{1,0:T(8,128)(2,1)S(1)} %pad_maximum_fusion.2), channel_id=1, source_target_pairs={{0,4},{2,6},{4,0},{6,2},{8,12},{10,14},{12,8},{14,10},{16,20},{18,... | collective-permute-start | bytes 448520 | tf_op jit(solution)/shard_map/ppermute | solution.py:391
  72.1 6.2 %collective-permute-start.25 = (bf16[288,128]{1,0:T(8,128)(2,1)S(1)}, bf16[288,128]{1,0:T(8,128)(2,1)S(1)}, u32[]{:S(2)}, u32[]{:S(2)}) collective-permute-start(bf16[288,128]{1,0:T(8,128)(2,1)S(1)} %get-tuple-element.216), channel_id=1, source_target_pairs={{0,16},{2,18},{4,20},{6,22},{8,24},{10,26},{12,28},{14,30},{16,0},... | collective-permute-start | bytes 221192 | tf_op jit(solution)/shard_map/ppermute | solution.py:391
  74.4 6.1 %collective-permute-start.26 = (bf16[288,128]{1,0:T(8,128)(2,1)S(1)}, bf16[288,128]{1,0:T(8,128)(2,1)S(1)}, u32[]{:S(2)}, u32[]{:S(2)}) collective-permute-start(bf16[288,128]{1,0:T(8,128)(2,1)S(1)} %get-tuple-element.225), channel_id=1, source_target_pairs={{0,16},{2,18},{4,20},{6,22},{8,24},{10,26},{12,28},{14,30},{16,0},... | collective-permute-start | bytes 221192 | tf_op jit(solution)/shard_map/ppermute | solution.py:391
  78.4 7.1 %collective-permute-start.21 = (bf16[1016,128]{1,0:T(8,128)(2,1)S(1)}, bf16[1016,128]{1,0:T(8,128)(2,1)S(1)}, u32[]{:S(2)}, u32[]{:S(2)}) collective-permute-start(bf16[1016,128]{1,0:T(8,128)(2,1)S(1)} %convert_dynamic-update-slice_fusion), channel_id=1, source_target_pairs={{0,2},{2,0},{4,6},{6,4},{8,10},{10,8},{12,14},{14,12},{16,18},{18,... | collective-permute-start | bytes 780296 | tf_op jit(solution)/shard_map/ppermute | solution.py:391
  80.6 4.8 %collective-permute-start.27 = (bf16[432,128]{1,0:T(8,128)(2,1)S(1)}, bf16[432,128]{1,0:T(8,128)(2,1)S(1)}, u32[]{:S(2)}, u32[]{:S(2)}) collective-permute-start(bf16[432,128]{1,0:T(8,128)(2,1)S(1)} %pad_maximum_fusion.3), channel_id=1, source_target_pairs={{0,4},{2,6},{4,0},{6,2},{8,12},{10,14},{12,8},{14,10},{16,20},{18,... | collective-permute-start | bytes 331784 | tf_op jit(solution)/shard_map/ppermute | solution.py:391
  85.4 1.5 %collective-permute-start.28 = (bf16[864,128]{1,0:T(8,128)(2,1)S(1)}, bf16[864,128]{1,0:T(8,128)(2,1)S(1)}, u32[]{:S(2)}, u32[]{:S(2)}) collective-permute-start(bf16[864,128]{1,0:T(8,128)(2,1)S(1)} %pad_maximum_fusion.1), channel_id=1, source_target_pairs={{0,2},{2,0},{4,6},{6,4},{8,10},{10,8},{12,14},{14,12},{16,18},{18,... | collective-permute-start | bytes 663560 | tf_op jit(solution)/shard_map/ppermute | solution.py:391

commit v2 on v1

--- a/solution.py
+++ b/solution.py
@@ -16,7 +16,7 @@
 PLAN = (1, 1, 1, 1, 1, 1)
 PAIR_PLAN = (1, 1, 1, 1, 1, 1)
 RIDING = 1
-EARLY = 3
+EARLY = 4
 WAIT = 0
 LAG = 3.1
 PACK = 4

time: 89.1 us -> 89.7 us (level)
  waiting for transfers between devices: 23.4 us -> 24.5 us
    ppermute x17, waiting for transfers between devices: 15.4 us -> 16.5 us  [flip(): return lax.ppermute(x, 'xy', [(i, i ^ bit) for i in range(tiles)])]
    unnamed x34 -> x36, local copies, waits for them, and re-layouts: 2.75 us -> 2.77 us
where the time goes in v2:
time: 89.7 us; the launch traced here: 89.2 us
  starting transfers between devices  34.5 us (38%)
  waiting for transfers between devices  24.5 us (27%)
  Pallas kernels  23.6 us (26%)
  local copies, waits for them, and re-layouts  4.65 us (5%)
  between operations  1.13 us (1%)
    ppermute x17, starting transfers between devices, flip(): return lax.ppermute(x, 'xy', [(i, i ^ bit) for i in range(tiles)])  18.4 us
    ppermute x17, waiting for transfers between devices, flip(): return lax.ppermute(x, 'xy', [(i, i ^ bit) for i in range(tiles)])  16.5 us
    ppermute x6, starting transfers between devices, to_slab(): lax.ppermute(x, 'gz', [(i, (i + step) % slabs) for i in range(slabs)])  9.23 us
    ppermute x6, waiting for transfers between devices, to_pair(): return lax.ppermute(x, 'xy', [(i, target(i)) for i in range(tiles)])  7.97 us
    pallas_call x1, Pallas kernels, modes(): pl.pallas_call(modes_kernel, grid_spec=pltpu.PrefetchScalarGridSpec(num_s...  6.98 us
    pallas_call x1, Pallas kernels, plane(): pl.pallas_call(functools.partial(plane_kernel, targets), grid_spec=pltpu....  6.89 us
    ppermute x6, starting transfers between devices, to_pair(): return lax.ppermute(x, 'xy', [(i, target(i)) for i in range(tiles)])  6.83 us
    pallas_call x6, Pallas kernels, along_x(): pl.pallas_call(functools.partial(along_x_kernel, tall, len(riders)), out_...  3.95 us
  transfers between devices with their start and end apart: 29, of which 13 were waited for; matrix products, arithmetic and copies ran while one was open for 3% of the time, Pallas kernels for 17%

profile of v2, /device:TPU:0, one launch (start us, length us, event | category | flops | bytes accessed | tf_op | source)
XLA Modules:
  0.0 89.2 jit_solution(16076622435164795730)
XLA Ops:
  0.6 0.5 collective-permute-start
  1.2 0.6 stack.20.tile.place
  1.8 7.0 %modes.1 = (f32[128,128]{1,0:T(8,128)}, f32[128,128]{1,0:T(8,128)}, f32[96,128]{1,0:T(8,128)}) custom-call(s32[5]{0:T(128)} %stack.20.tile.place, bf16[128,128,128]{2,1,0:T(8,128)(2,1)} %bitcast.38, bf16[128,128,128]{2,1,0:T(8,128)(2,1)} %bitcast.39, bf16[96,128]{1,0:T(8,128)(2,1)} %bitcast.59, bf16[96,128]{1,0:T(8,128)(2,1)} %bitcast.60, ...), custom_call_target="tpu_custom_call" | custom-call | flops 1476395008 | bytes 4194304 | tf_op jit(solution)/shard_map/modes/pallas_call | solution.py:74
  8.9 6.9 %plane.1 = (bf16[128,8,128]{2,1,0:T(8,128)(2,1)}, bf16[128,8,128]{2,1,0:T(8,128)(2,1)}, bf16[128,8,128]{2,1,0:T(8,128)(2,1)}, bf16[128,8,128]{2,1,0:T(8,128)(2,1...) custom-call(s32[5]{0:T(128)} %stack.20.tile.place, ...), custom_call_target="tpu_custom_call" | custom-call | flops 805306368 | bytes 12582912 | tf_op jit(solution)/shard_map/plane/pallas_call | solution.py:148
  15.8 2.7 %collective-permute-start.1 = (bf16[128,8,128]{2,1,0:T(8,128)(2,1)}, bf16[128,8,128]{2,1,0:T(8,128)(2,1)S(1)}, u32[]{:S(2)}, u32[]{:S(2)}) collective-permute-start(bf16[128,8,128]{2,1,0:T(8,128)(2,1)} %get-tuple-element.123), channel_id=1, source_target_pairs={{0,4},{2,6},{4,0},{6,2},{8,12},{10,14},{12,8},{14,10},{16,20},{18,... | collective-permute-start | bytes 786440 | tf_op jit(solution)/shard_map/ppermute | solution.py:398
  19.9 1.9 %collective-permute-start.4 = (bf16[128,8,128]{2,1,0:T(8,128)(2,1)S(1)}, bf16[128,8,128]{2,1,0:T(8,128)(2,1)S(1)}, u32[]{:S(2)}, u32[]{:S(2)}) collective-permute-start(bf16[128,8,128]{2,1,0:T(8,128)(2,1)S(1)} %copy-done.14), channel_id=1, source_target_pairs={{0,4},{2,6},{4,0},{6,2},{8,12},{10,14},{12,8},{14,10},{16,20},{18,... | collective-permute-start | bytes 786440 | tf_op jit(solution)/shard_map/ppermute | solution.py:398
  22.0 3.8 %collective-permute-done.1.refs_0_ = bf16[128,8,128]{2,1,0:T(8,128)(2,1)S(1)} collective-permute-done((bf16[128,8,128]{2,1,0:T(8,128)(2,1)}, bf16[128,8,128]{2,1,0:T(8,128)(2,1)S(1)}, u32[]{:S(2)}, u32[]{:S(2)}) %collective-permute-start.1) | collective-permute-done | bytes 262176 | tf_op jit(solution)/shard_map/ppermute | solution.py:398
  26.2 2.1 %collective-permute-start.3 = (bf16[768,128]{1,0:T(8,128)(2,1)S(1)}, bf16[768,128]{1,0:T(8,128)(2,1)S(1)}, u32[]{:S(2)}, u32[]{:S(2)}) collective-permute-start(bf16[768,128]{1,0:T(8,128)(2,1)S(1)} %get-tuple-element.127), channel_id=1, source_target_pairs={{0,1},{1,0},{2,3},{3,2},{4,5},{5,4},{6,7},{7,6},{8,9},{9,8},{10,11... | collective-permute-start | bytes 589832 | tf_op jit(solution)/shard_map/ppermute | solution.py:403
  28.3 3.1 %collective-permute-done.2.refs_0_ = bf16[128,8,128]{2,1,0:T(8,128)(2,1)S(1)} collective-permute-done((bf16[128,8,128]{2,1,0:T(8,128)(2,1)}, bf16[128,8,128]{2,1,0:T(8,128)(2,1)S(1)}, u32[]{:S(2)}, u32[]{:S(2)}) %collective-permute-start.2) | collective-permute-done | bytes 262176 | tf_op jit(solution)/shard_map/ppermute | solution.py:398
  31.9 2.1 %collective-permute-start.5 = (bf16[1024,128]{1,0:T(8,128)(2,1)S(1)}, bf16[1024,128]{1,0:T(8,128)(2,1)S(1)}, u32[]{:S(2)}, u32[]{:S(2)}) collective-permute-start(bf16[1024,128]{1,0:T(8,128)(2,1)S(1)} %get-tuple-element.133), channel_id=1, source_target_pairs={{0,1},{1,0},{2,3},{3,2},{4,5},{5,4},{6,7},{7,6},{8,9},{9,8},{10,11... | collective-permute-start | bytes 786440 | tf_op jit(solution)/shard_map/ppermute | solution.py:403
  34.4 1.6 %collective-permute-start.7 = (bf16[576,128]{1,0:T(8,128)(2,1)S(1)}, bf16[576,128]{1,0:T(8,128)(2,1)S(1)}, u32[]{:S(2)}, u32[]{:S(2)}) collective-permute-start(bf16[576,128]{1,0:T(8,128)(2,1)S(1)} %get-tuple-element.138), channel_id=1, source_target_pairs={{0,8},{2,10},{4,12},{6,14},{8,0},{10,2},{12,4},{14,6},{16,24},{18,... | collective-permute-start | bytes 442376 | tf_op jit(solution)/shard_map/ppermute | solution.py:391
  36.1 1.0 %collective-permute-done.4.refs_0_ = bf16[128,8,128]{2,1,0:T(8,128)(2,1)S(1)} collective-permute-done((bf16[128,8,128]{2,1,0:T(8,128)(2,1)S(1)}, bf16[128,8,128]{2,1,0:T(8,128)(2,1)S(1)}, u32[]{:S(2)}, u32[]{:S(2)}) %collective-permute-start.4) | collective-permute-done | bytes 262176 | tf_op jit(solution)/shard_map/ppermute | solution.py:398
  37.1 1.1 %along_z.8 = (f32[768,128]{1,0:T(8,128)S(1)}, bf16[768,128]{1,0:T(8,128)(2,1)}) custom-call(bf16[128,8,128]{2,1,0:T(8,128)(2,1)S(1)} %copy-done.4, bf16[128,8,128]{2,1,0:T(8,128)(2,1)S(1)} %collective-permute-done.4.refs_0_, bf16[512,768]{1,0:T(8,128)(2,1)S(1)} %pad_maximum_fusion.refs_1_), custom_call_target="tpu_custom_call" | custom-call | flops 201326592 | bytes 1048576 | tf_op jit(solution)/shard_map/along_z/pallas_call | solution.py:204
  38.2 2.0 %collective-permute-start.8 = (bf16[768,128]{1,0:T(8,128)(2,1)}, bf16[768,128]{1,0:T(8,128)(2,1)}, u32[]{:S(2)}, u32[]{:S(2)}) collective-permute-start(bf16[768,128]{1,0:T(8,128)(2,1)} %get-tuple-element.143), channel_id=1, source_target_pairs={{0,1},{1,0},{2,3},{3,2},{4,5},{5,4},{6,7},{7,6},{8,9},{9,8},{10,11... | collective-permute-start | bytes 589832 | tf_op jit(solution)/shard_map/ppermute | solution.py:403
  40.2 1.5 %collective-permute-start.9 = (bf16[128,8,128]{2,1,0:T(8,128)(2,1)}, bf16[128,8,128]{2,1,0:T(8,128)(2,1)S(1)}, u32[]{:S(2)}, u32[]{:S(2)}) collective-permute-start(bf16[128,8,128]{2,1,0:T(8,128)(2,1)} %get-tuple-element.164), channel_id=1, source_target_pairs={{0,4},{2,6},{4,0},{6,2},{8,12},{10,14},{12,8},{14,10},{16,20},{18,... | collective-permute-start | bytes 786440 | tf_op jit(solution)/shard_map/ppermute | solution.py:398
  41.7 0.5 collective-permute-start.13
  42.2 0.9 %along_x.7 = (f32[800,128]{1,0:T(8,128)S(1)}, bf16[800,128]{1,0:T(8,128)(2,1)}, f32[128,128]{1,0:T(8,128)S(1)}) custom-call(f32[1024,128]{1,0:T(8,128)S(1)} %get-tuple-element.145.near, bf16[1024,128]{1,0:T(8,128)(2,1)S(1)} %collective-permute-done.5.refs_0_, bf16[192,128]{1,0:T(8,128)(2,1)S(1)} %convolution_convert_fusion.refs_1_, f32[96,128]{1,0:T(8,128)S(1)} %copy-done.11), custom_call_target="tpu_custom_call" | custom-call | flops 37748736 | bytes 589824 | tf_op jit(solution)/shard_map/along_x/pallas_call | solution.py:253
  43.1 0.6 copy-done.12
  43.7 1.6 %collective-permute-start.10 = (bf16[800,128]{1,0:T(8,128)(2,1)}, bf16[800,128]{1,0:T(8,128)(2,1)S(1)}, u32[]{:S(2)}, u32[]{:S(2)}) collective-permute-start(bf16[800,128]{1,0:T(8,128)(2,1)} %get-tuple-element.149), channel_id=1, source_target_pairs={{0,8},{2,10},{4,12},{6,14},{8,0},{10,2},{12,4},{14,6},{16,24},{18,... | collective-permute-start | bytes 614408 | tf_op jit(solution)/shard_map/ppermute | solution.py:391
  45.3 1.1 %along_z.9 = (f32[768,128]{1,0:T(8,128)S(1)}, bf16[768,128]{1,0:T(8,128)(2,1)}) custom-call(bf16[128,8,128]{2,1,0:T(8,128)(2,1)S(1)} %copy-done.3, bf16[128,8,128]{2,1,0:T(8,128)(2,1)S(1)} %collective-permute-done.6.refs_0_, bf16[512,768]{1,0:T(8,128)(2,1)S(1)} %pad_maximum_fusion.refs_1_), custom_call_target="tpu_custom_call" | custom-call | flops 201326592 | bytes 1048576 | tf_op jit(solution)/shard_map/along_z/pallas_call | solution.py:204
  46.4 0.7 copy-done.7
  47.1 0.9 %collective-permute-start.11 = (bf16[768,128]{1,0:T(8,128)(2,1)}, bf16[768,128]{1,0:T(8,128)(2,1)}, u32[]{:S(2)}, u32[]{:S(2)}) collective-permute-start(bf16[768,128]{1,0:T(8,128)(2,1)} %get-tuple-element.154), channel_id=1, source_target_pairs={{0,1},{1,0},{2,3},{3,2},{4,5},{5,4},{6,7},{7,6},{8,9},{9,8},{10,11... | collective-permute-start | bytes 589832 | tf_op jit(solution)/shard_map/ppermute | solution.py:403
  48.0 0.9 %copy-done.8 = bf16[576,128]{1,0:T(8,128)(2,1)S(1)} copy-done((bf16[576,128]{1,0:T(8,128)(2,1)S(1)}, bf16[576,128]{1,0:T(8,128)(2,1)}, u32[]{:S(2)}) %copy-start.8) | copy-done | bytes 147480
  49.0 2.7 %collective-permute-start.12 = (bf16[288,128]{1,0:T(8,128)(2,1)S(1)}, bf16[288,128]{1,0:T(8,128)(2,1)S(1)}, u32[]{:S(2)}, u32[]{:S(2)}) collective-permute-start(bf16[288,128]{1,0:T(8,128)(2,1)S(1)} %get-tuple-element.158), channel_id=1, source_target_pairs={{0,16},{2,18},{4,20},{6,22},{8,24},{10,26},{12,28},{14,30},{16,0},... | collective-permute-start | bytes 221192 | tf_op jit(solution)/shard_map/ppermute | solution.py:391
  51.6 0.8 constant_dynamic-slice_fusion.1
  52.4 1.2 %along_x.8 = (f32[576,128]{1,0:T(8,128)S(1)}, bf16[576,128]{1,0:T(8,128)(2,1)S(1)}) custom-call(f32[768,128]{1,0:T(8,128)S(1)} %get-tuple-element.160.near, bf16[768,128]{1,0:T(8,128)(2,1)} %collective-permute-done.8.refs_0_, bf16[192,128]{1,0:T(8,128)(2,1)S(1)} %convolution_convert_fusion.refs_1_), custom_call_target="tpu_custom_call" | custom-call | flops 37748736 | bytes 589824 | tf_op jit(solution)/shard_map/along_x/pallas_call | solution.py:253
  53.6 0.5 collective-permute-start.14
  54.6 1.1 %collective-permute-start.15 = (bf16[768,128]{1,0:T(8,128)(2,1)S(1)}, bf16[768,128]{1,0:T(8,128)(2,1)S(1)}, u32[]{:S(2)}, u32[]{:S(2)}) collective-permute-start(bf16[768,128]{1,0:T(8,128)(2,1)S(1)} %get-tuple-element.167), channel_id=1, source_target_pairs={{0,1},{1,0},{2,3},{3,2},{4,5},{5,4},{6,7},{7,6},{8,9},{9,8},{10,11... | collective-permute-start | bytes 589832 | tf_op jit(solution)/shard_map/ppermute | solution.py:403
  56.2 1.2 %along_x.9 = (f32[576,128]{1,0:T(8,128)S(1)}, bf16[576,128]{1,0:T(8,128)(2,1)S(1)}) custom-call(f32[768,128]{1,0:T(8,128)S(1)} %get-tuple-element.173.near, bf16[768,128]{1,0:T(8,128)(2,1)} %collective-permute-done.11.refs_0_, bf16[192,128]{1,0:T(8,128)(2,1)S(1)} %convolution_convert_fusion.refs_1_), custom_call_target="tpu_custom_call" | custom-call | flops 37748736 | bytes 589824 | tf_op jit(solution)/shard_map/along_x/pallas_call | solution.py:253
  57.3 1.6 %collective-permute-start.17 = (bf16[576,128]{1,0:T(8,128)(2,1)S(1)}, bf16[576,128]{1,0:T(8,128)(2,1)S(1)}, u32[]{:S(2)}, u32[]{:S(2)}) collective-permute-start(bf16[576,128]{1,0:T(8,128)(2,1)S(1)} %get-tuple-element.175), channel_id=1, source_target_pairs={{0,8},{2,10},{4,12},{6,14},{8,0},{10,2},{12,4},{14,6},{16,24},{18,... | collective-permute-start | bytes 442376 | tf_op jit(solution)/shard_map/ppermute | solution.py:391
  59.4 1.0 %collective-permute-start.18 = (bf16[768,128]{1,0:T(8,128)(2,1)S(1)}, bf16[768,128]{1,0:T(8,128)(2,1)S(1)}, u32[]{:S(2)}, u32[]{:S(2)}) collective-permute-start(bf16[768,128]{1,0:T(8,128)(2,1)S(1)} %get-tuple-element.184), channel_id=1, source_target_pairs={{0,1},{1,0},{2,3},{3,2},{4,5},{5,4},{6,7},{7,6},{8,9},{9,8},{10,11... | collective-permute-start | bytes 589832 | tf_op jit(solution)/shard_map/ppermute | solution.py:403
  60.5 2.0 %collective-permute-done.14.far = bf16[576,128]{1,0:T(8,128)(2,1)S(1)} collective-permute-done((bf16[576,128]{1,0:T(8,128)(2,1)S(1)}, bf16[576,128]{1,0:T(8,128)(2,1)S(1)}, u32[]{:S(2)}, u32[]{:S(2)}) %collective-permute-start.14) | collective-permute-done | bytes 147488 | tf_op jit(solution)/shard_map/ppermute | solution.py:391
  62.5 0.7 collective-permute-start.19
  64.5 2.2 %collective-permute-done.17.far = bf16[576,128]{1,0:T(8,128)(2,1)S(1)} collective-permute-done((bf16[576,128]{1,0:T(8,128)(2,1)S(1)}, bf16[576,128]{1,0:T(8,128)(2,1)S(1)}, u32[]{:S(2)}, u32[]{:S(2)}) %collective-permute-start.17) | collective-permute-done | bytes 147488 | tf_op jit(solution)/shard_map/ppermute | solution.py:391
  66.8 1.3 %collective-permute-start.21 = (bf16[288,128]{1,0:T(8,128)(2,1)S(1)}, bf16[288,128]{1,0:T(8,128)(2,1)S(1)}, u32[]{:S(2)}, u32[]{:S(2)}) collective-permute-start(bf16[288,128]{1,0:T(8,128)(2,1)S(1)} %get-tuple-element.201), channel_id=1, source_target_pairs={{0,16},{2,18},{4,20},{6,22},{8,24},{10,26},{12,28},{14,30},{16,0},... | collective-permute-start | bytes 221192 | tf_op jit(solution)/shard_map/ppermute | solution.py:391
  68.3 1.7 %collective-permute-start.24 = (bf16[576,128]{1,0:T(8,128)(2,1)S(1)}, bf16[576,128]{1,0:T(8,128)(2,1)S(1)}, u32[]{:S(2)}, u32[]{:S(2)}) collective-permute-start(bf16[576,128]{1,0:T(8,128)(2,1)S(1)} %get-tuple-element.205), channel_id=1, source_target_pairs={{0,8},{2,10},{4,12},{6,14},{8,0},{10,2},{12,4},{14,6},{16,24},{18,... | collective-permute-start | bytes 442376 | tf_op jit(solution)/shard_map/ppermute | solution.py:391
  70.1 2.0 %collective-permute-done.20.far = bf16[576,128]{1,0:T(8,128)(2,1)S(1)} collective-permute-done((bf16[576,128]{1,0:T(8,128)(2,1)S(1)}, bf16[576,128]{1,0:T(8,128)(2,1)S(1)}, u32[]{:S(2)}, u32[]{:S(2)}) %collective-permute-start.20) | collective-permute-done | bytes 147488 | tf_op jit(solution)/shard_map/ppermute | solution.py:391
  72.2 0.6 collective-permute-start.25
  72.8 1.3 %collective-permute-done.21.far = bf16[288,128]{1,0:T(8,128)(2,1)S(1)} collective-permute-done((bf16[288,128]{1,0:T(8,128)(2,1)S(1)}, bf16[288,128]{1,0:T(8,128)(2,1)S(1)}, u32[]{:S(2)}, u32[]{:S(2)}) %collective-permute-start.21) | collective-permute-done | bytes 73760 | tf_op jit(solution)/shard_map/ppermute | solution.py:391
  74.1 1.5 %collective-permute-start.22 = (bf16[728,128]{1,0:T(8,128)(2,1)S(1)}, bf16[728,128]{1,0:T(8,128)(2,1)S(1)}, u32[]{:S(2)}, u32[]{:S(2)}) collective-permute-start(bf16[728,128]{1,0:T(8,128)(2,1)S(1)} %fusion.3), channel_id=1, source_target_pairs={{0,4},{2,6},{4,0},{6,2},{8,12},{10,14},{12,8},{14,10},{16,20},{18,... | collective-permute-start | bytes 559112 | tf_op jit(solution)/shard_map/ppermute | solution.py:391
  75.6 1.3 %collective-permute-start.26 = (bf16[288,128]{1,0:T(8,128)(2,1)S(1)}, bf16[288,128]{1,0:T(8,128)(2,1)S(1)}, u32[]{:S(2)}, u32[]{:S(2)}) collective-permute-start(bf16[288,128]{1,0:T(8,128)(2,1)S(1)} %get-tuple-element.225), channel_id=1, source_target_pairs={{0,16},{2,18},{4,20},{6,22},{8,24},{10,26},{12,28},{14,30},{16,0},... | collective-permute-start | bytes 221192 | tf_op jit(solution)/shard_map/ppermute | solution.py:391
  76.9 1.4 %collective-permute-done.25.far = bf16[288,128]{1,0:T(8,128)(2,1)S(1)} collective-permute-done((bf16[288,128]{1,0:T(8,128)(2,1)S(1)}, bf16[288,128]{1,0:T(8,128)(2,1)S(1)}, u32[]{:S(2)}, u32[]{:S(2)}) %collective-permute-start.25) | collective-permute-done | bytes 73760 | tf_op jit(solution)/shard_map/ppermute | solution.py:391
  78.3 2.8 %collective-permute-done.26.far = bf16[288,128]{1,0:T(8,128)(2,1)S(1)} collective-permute-done((bf16[288,128]{1,0:T(8,128)(2,1)S(1)}, bf16[288,128]{1,0:T(8,128)(2,1)S(1)}, u32[]{:S(2)}, u32[]{:S(2)}) %collective-permute-start.26) | collective-permute-done | bytes 73760 | tf_op jit(solution)/shard_map/ppermute | solution.py:391
  81.2 1.2 %collective-permute-start.27 = (bf16[288,128]{1,0:T(8,128)(2,1)S(1)}, bf16[288,128]{1,0:T(8,128)(2,1)S(1)}, u32[]{:S(2)}, u32[]{:S(2)}) collective-permute-start(bf16[288,128]{1,0:T(8,128)(2,1)S(1)} %pad_maximum_fusion.4), channel_id=1, source_target_pairs={{0,4},{2,6},{4,0},{6,2},{8,12},{10,14},{12,8},{14,10},{16,20},{18,... | collective-permute-start | bytes 221192 | tf_op jit(solution)/shard_map/ppermute | solution.py:391
  82.5 3.1 %collective-permute-done.27 = bf16[288,128]{1,0:T(8,128)(2,1)S(1)} collective-permute-done((bf16[288,128]{1,0:T(8,128)(2,1)S(1)}, bf16[288,128]{1,0:T(8,128)(2,1)S(1)}, u32[]{:S(2)}, u32[]{:S(2)}) %collective-permute-start.27) | collective-permute-done | bytes 73760 | tf_op jit(solution)/shard_map/ppermute | solution.py:391
  85.7 0.6 collective-permute-start.23
  86.3 0.8 collective-permute-done.28
  87.6 1.6 %unpack.1 = (f32[16,96]{1,0:T(8,128)}, f32[16,96]{1,0:T(8,128)}, f32[6,128]{1,0:T(8,128)}, f32[12,192,96]{2,1,0:T(8,128)}) custom-call(s32[1]{0:T(128)} %bitcast.column, f32[152,128]{1,0:T(8,128)S(1)} %convert_add_fusion.sketches, bf16[2304,128]{1,0:T(8,128)(2,1)S(1)} %slice_dynamic-update-slice_fusion.refs_0_, bf16[1152,128]{1,0:T(8,128)(2,1)S(1)} %pad_maximum_fusion.1.refs_1_), custom_call_target="tpu_custom_call" | custom-call | flops 1179648 | bytes 2359296 | tf_op jit(solution)/shard_map/unpack/pallas_call | solution.py:332
  (101 shorter events, 6.7 us)
Async XLA Ops:
  0.6 33.3 %copy-start = (bf16[512,192]{0,1:T(8,128)(2,1)S(1)}, bf16[512,192]{0,1:T(8,128)(2,1)}, u32[]{:S(2)}) copy-start(bf16[512,192]{0,1:T(8,128)(2,1)} %param.12) | copy-start | bytes 589828
  0.6 8.2 %collective-permute-start = (bf16[128,128,128]{2,1,0:T(8,128)(2,1)}, bf16[128,128,128]{2,1,0:T(8,128)(2,1)}, u32[]{:S(2)}, u32[]{:S(2)}) collective-permute-start(bf16[128,128,128]{2,1,0:T(8,128)(2,1)} %bitcast.37), channel_id=1, source_target_pairs={{0,2},{2,0},{4,6},{6,4},{8,10},{10,8},{12,14},{14,12},{16,18},{18,... | collective-permute-start | bytes 12582920 | tf_op jit(solution)/shard_map/ppermute | solution.py:391
  8.9 9.7 %copy-start.13 = (bf16[128,192]{0,1:T(8,128)(2,1)S(1)}, bf16[128,192]{0,1:T(8,128)(2,1)}, u32[]{:S(2)}) copy-start(bf16[128,192]{0,1:T(8,128)(2,1)} %param.14) | copy-start | bytes 147460
  15.8 10.1 %collective-permute-start.1 = (bf16[128,8,128]{2,1,0:T(8,128)(2,1)}, bf16[128,8,128]{2,1,0:T(8,128)(2,1)S(1)}, u32[]{:S(2)}, u32[]{:S(2)}) collective-permute-start(bf16[128,8,128]{2,1,0:T(8,128)(2,1)} %get-tuple-element.123), channel_id=1, source_target_pairs={{0,4},{2,6},{4,0},{6,2},{8,12},{10,14},{12,8},{14,10},{16,20},{18,... | collective-permute-start | bytes 786440 | tf_op jit(solution)/shard_map/ppermute | solution.py:398
  18.5 13.0 %collective-permute-start.2 = (bf16[128,8,128]{2,1,0:T(8,128)(2,1)}, bf16[128,8,128]{2,1,0:T(8,128)(2,1)S(1)}, u32[]{:S(2)}, u32[]{:S(2)}) collective-permute-start(bf16[128,8,128]{2,1,0:T(8,128)(2,1)} %get-tuple-element.129), channel_id=1, source_target_pairs={{0,4},{2,6},{4,0},{6,2},{8,12},{10,14},{12,8},{14,10},{16,20},{18,... | collective-permute-start | bytes 786440 | tf_op jit(solution)/shard_map/ppermute | solution.py:398
  18.9 1.0 %copy-start.14 = (bf16[128,8,128]{2,1,0:T(8,128)(2,1)S(1)}, bf16[128,8,128]{2,1,0:T(8,128)(2,1)}, u32[]{:S(2)}) copy-start(bf16[128,8,128]{2,1,0:T(8,128)(2,1)} %get-tuple-element.140) | copy-start | bytes 786436
  19.2 6.6 %copy-start.5 = (bf16[128,8,128]{2,1,0:T(8,128)(2,1)S(1)}, bf16[128,8,128]{2,1,0:T(8,128)(2,1)}, u32[]{:S(2)}) copy-start(bf16[128,8,128]{2,1,0:T(8,128)(2,1)} %get-tuple-element.124.near) | copy-start | bytes 786436
  19.5 11.9 %copy-start.6 = (bf16[128,8,128]{2,1,0:T(8,128)(2,1)S(1)}, bf16[128,8,128]{2,1,0:T(8,128)(2,1)}, u32[]{:S(2)}) copy-start(bf16[128,8,128]{2,1,0:T(8,128)(2,1)} %get-tuple-element.130.near) | copy-start | bytes 786436
  19.5 11.9 %copy-start.9 = (f32[128,128]{1,0:T(8,128)S(1)}, f32[128,128]{1,0:T(8,128)}, u32[]{:S(2)}) copy-start(f32[128,128]{1,0:T(8,128)} %get-tuple-element.120.refs_2_) | copy-start | bytes 196612
  19.5 11.9 %copy-start.10 = (f32[128,128]{1,0:T(8,128)S(1)}, f32[128,128]{1,0:T(8,128)}, u32[]{:S(2)}) copy-start(f32[128,128]{1,0:T(8,128)} %get-tuple-element.132.refs_3_) | copy-start | bytes 196612
  19.9 17.2 %collective-permute-start.4 = (bf16[128,8,128]{2,1,0:T(8,128)(2,1)S(1)}, bf16[128,8,128]{2,1,0:T(8,128)(2,1)S(1)}, u32[]{:S(2)}, u32[]{:S(2)}) collective-permute-start(bf16[128,8,128]{2,1,0:T(8,128)(2,1)S(1)} %copy-done.14), channel_id=1, source_target_pairs={{0,4},{2,6},{4,0},{6,2},{8,12},{10,14},{12,8},{14,10},{16,20},{18,... | collective-permute-start | bytes 786440 | tf_op jit(solution)/shard_map/ppermute | solution.py:398
  21.8 21.9 %collective-permute-start.6 = (bf16[128,8,128]{2,1,0:T(8,128)(2,1)}, bf16[128,8,128]{2,1,0:T(8,128)(2,1)S(1)}, u32[]{:S(2)}, u32[]{:S(2)}) collective-permute-start(bf16[128,8,128]{2,1,0:T(8,128)(2,1)} %get-tuple-element.151), channel_id=1, source_target_pairs={{0,4},{2,6},{4,0},{6,2},{8,12},{10,14},{12,8},{14,10},{16,20},{18,... | collective-permute-start | bytes 786440 | tf_op jit(solution)/shard_map/ppermute | solution.py:398
  22.0 15.1 %copy-start.4 = (bf16[128,8,128]{2,1,0:T(8,128)(2,1)S(1)}, bf16[128,8,128]{2,1,0:T(8,128)(2,1)}, u32[]{:S(2)}) copy-start(bf16[128,8,128]{2,1,0:T(8,128)(2,1)} %get-tuple-element.141.near) | copy-start | bytes 786436
  26.2 8.0 %collective-permute-start.3 = (bf16[768,128]{1,0:T(8,128)(2,1)S(1)}, bf16[768,128]{1,0:T(8,128)(2,1)S(1)}, u32[]{:S(2)}, u32[]{:S(2)}) collective-permute-start(bf16[768,128]{1,0:T(8,128)(2,1)S(1)} %get-tuple-element.127), channel_id=1, source_target_pairs={{0,1},{1,0},{2,3},{3,2},{4,5},{5,4},{6,7},{7,6},{8,9},{9,8},{10,11... | collective-permute-start | bytes 589832 | tf_op jit(solution)/shard_map/ppermute | solution.py:403
  31.5 10.7 %copy-start.11 = (f32[96,128]{1,0:T(8,128)S(1)}, f32[96,128]{1,0:T(8,128)}, u32[]{:S(2)}) copy-start(f32[96,128]{1,0:T(8,128)} %get-tuple-element.147.refs_2_) | copy-start | bytes 147460
  31.9 13.4 %copy-start.3 = (bf16[128,8,128]{2,1,0:T(8,128)(2,1)S(1)}, bf16[128,8,128]{2,1,0:T(8,128)(2,1)}, u32[]{:S(2)}) copy-start(bf16[128,8,128]{2,1,0:T(8,128)(2,1)} %get-tuple-element.152.near) | copy-start | bytes 786436
  31.9 9.8 %collective-permute-start.5 = (bf16[1024,128]{1,0:T(8,128)(2,1)S(1)}, bf16[1024,128]{1,0:T(8,128)(2,1)S(1)}, u32[]{:S(2)}, u32[]{:S(2)}) collective-permute-start(bf16[1024,128]{1,0:T(8,128)(2,1)S(1)} %get-tuple-element.133), channel_id=1, source_target_pairs={{0,1},{1,0},{2,3},{3,2},{4,5},{5,4},{6,7},{7,6},{8,9},{9,8},{10,11... | collective-permute-start | bytes 786440 | tf_op jit(solution)/shard_map/ppermute | solution.py:403
  34.4 12.0 %collective-permute-start.7 = (bf16[576,128]{1,0:T(8,128)(2,1)S(1)}, bf16[576,128]{1,0:T(8,128)(2,1)S(1)}, u32[]{:S(2)}, u32[]{:S(2)}) collective-permute-start(bf16[576,128]{1,0:T(8,128)(2,1)S(1)} %get-tuple-element.138), channel_id=1, source_target_pairs={{0,8},{2,10},{4,12},{6,14},{8,0},{10,2},{12,4},{14,6},{16,24},{18,... | collective-permute-start | bytes 442376 | tf_op jit(solution)/shard_map/ppermute | solution.py:391
  38.2 10.8 %collective-permute-start.8 = (bf16[768,128]{1,0:T(8,128)(2,1)}, bf16[768,128]{1,0:T(8,128)(2,1)}, u32[]{:S(2)}, u32[]{:S(2)}) collective-permute-start(bf16[768,128]{1,0:T(8,128)(2,1)} %get-tuple-element.143), channel_id=1, source_target_pairs={{0,1},{1,0},{2,3},{3,2},{4,5},{5,4},{6,7},{7,6},{8,9},{9,8},{10,11... | collective-permute-start | bytes 589832 | tf_op jit(solution)/shard_map/ppermute | solution.py:403
  40.2 13.4 %collective-permute-start.9 = (bf16[128,8,128]{2,1,0:T(8,128)(2,1)}, bf16[128,8,128]{2,1,0:T(8,128)(2,1)S(1)}, u32[]{:S(2)}, u32[]{:S(2)}) collective-permute-start(bf16[128,8,128]{2,1,0:T(8,128)(2,1)} %get-tuple-element.164), channel_id=1, source_target_pairs={{0,4},{2,6},{4,0},{6,2},{8,12},{10,14},{12,8},{14,10},{16,20},{18,... | collective-permute-start | bytes 786440 | tf_op jit(solution)/shard_map/ppermute | solution.py:398
  41.7 17.3 %collective-permute-start.13 = (bf16[128,8,128]{2,1,0:T(8,128)(2,1)}, bf16[128,8,128]{2,1,0:T(8,128)(2,1)S(1)}, u32[]{:S(2)}, u32[]{:S(2)}) collective-permute-start(bf16[128,8,128]{2,1,0:T(8,128)(2,1)} %get-tuple-element.181), channel_id=1, source_target_pairs={{0,4},{2,6},{4,0},{6,2},{8,12},{10,14},{12,8},{14,10},{16,20},{18,... | collective-permute-start | bytes 786440 | tf_op jit(solution)/shard_map/ppermute | solution.py:398
  42.2 11.9 %copy-start.2 = (bf16[128,8,128]{2,1,0:T(8,128)(2,1)S(1)}, bf16[128,8,128]{2,1,0:T(8,128)(2,1)}, u32[]{:S(2)}) copy-start(bf16[128,8,128]{2,1,0:T(8,128)(2,1)} %get-tuple-element.165.near) | copy-start | bytes 786436
  43.1 0.6 copy-start.12
  43.7 10.8 %collective-permute-start.10 = (bf16[800,128]{1,0:T(8,128)(2,1)}, bf16[800,128]{1,0:T(8,128)(2,1)S(1)}, u32[]{:S(2)}, u32[]{:S(2)}) collective-permute-start(bf16[800,128]{1,0:T(8,128)(2,1)} %get-tuple-element.149), channel_id=1, source_target_pairs={{0,8},{2,10},{4,12},{6,14},{8,0},{10,2},{12,4},{14,6},{16,24},{18,... | collective-permute-start | bytes 614408 | tf_op jit(solution)/shard_map/ppermute | solution.py:391
  46.4 0.7 copy-start.7
  47.1 8.7 %collective-permute-start.11 = (bf16[768,128]{1,0:T(8,128)(2,1)}, bf16[768,128]{1,0:T(8,128)(2,1)}, u32[]{:S(2)}, u32[]{:S(2)}) collective-permute-start(bf16[768,128]{1,0:T(8,128)(2,1)} %get-tuple-element.154), channel_id=1, source_target_pairs={{0,1},{1,0},{2,3},{3,2},{4,5},{5,4},{6,7},{7,6},{8,9},{9,8},{10,11... | collective-permute-start | bytes 589832 | tf_op jit(solution)/shard_map/ppermute | solution.py:403
  48.0 0.9 %copy-start.8 = (bf16[576,128]{1,0:T(8,128)(2,1)S(1)}, bf16[576,128]{1,0:T(8,128)(2,1)}, u32[]{:S(2)}) copy-start(bf16[576,128]{1,0:T(8,128)(2,1)} %copy-done.7) | copy-start | bytes 442372
  49.0 8.3 %collective-permute-start.12 = (bf16[288,128]{1,0:T(8,128)(2,1)S(1)}, bf16[288,128]{1,0:T(8,128)(2,1)S(1)}, u32[]{:S(2)}, u32[]{:S(2)}) collective-permute-start(bf16[288,128]{1,0:T(8,128)(2,1)S(1)} %get-tuple-element.158), channel_id=1, source_target_pairs={{0,16},{2,18},{4,20},{6,22},{8,24},{10,26},{12,28},{14,30},{16,0},... | collective-permute-start | bytes 221192 | tf_op jit(solution)/shard_map/ppermute | solution.py:391
  52.4 6.6 %copy-start.1 = (bf16[128,8,128]{2,1,0:T(8,128)(2,1)S(1)}, bf16[128,8,128]{2,1,0:T(8,128)(2,1)}, u32[]{:S(2)}) copy-start(bf16[128,8,128]{2,1,0:T(8,128)(2,1)} %get-tuple-element.182.near) | copy-start | bytes 786436
  53.6 8.8 %collective-permute-start.14 = (bf16[576,128]{1,0:T(8,128)(2,1)S(1)}, bf16[576,128]{1,0:T(8,128)(2,1)S(1)}, u32[]{:S(2)}, u32[]{:S(2)}) collective-permute-start(bf16[576,128]{1,0:T(8,128)(2,1)S(1)} %get-tuple-element.162), channel_id=1, source_target_pairs={{0,8},{2,10},{4,12},{6,14},{8,0},{10,2},{12,4},{14,6},{16,24},{18,... | collective-permute-start | bytes 442376 | tf_op jit(solution)/shard_map/ppermute | solution.py:391
  54.6 8.6 %collective-permute-start.15 = (bf16[768,128]{1,0:T(8,128)(2,1)S(1)}, bf16[768,128]{1,0:T(8,128)(2,1)S(1)}, u32[]{:S(2)}, u32[]{:S(2)}) collective-permute-start(bf16[768,128]{1,0:T(8,128)(2,1)S(1)} %get-tuple-element.167), channel_id=1, source_target_pairs={{0,1},{1,0},{2,3},{3,2},{4,5},{5,4},{6,7},{7,6},{8,9},{9,8},{10,11... | collective-permute-start | bytes 589832 | tf_op jit(solution)/shard_map/ppermute | solution.py:403
  55.8 8.6 %collective-permute-start.16 = (bf16[512,128]{1,0:T(8,128)(2,1)S(1)}, bf16[512,128]{1,0:T(8,128)(2,1)S(1)}, u32[]{:S(2)}, u32[]{:S(2)}) collective-permute-start(bf16[512,128]{1,0:T(8,128)(2,1)S(1)} %get-tuple-element.171), channel_id=1, source_target_pairs={{0,16},{2,18},{4,20},{6,22},{8,24},{10,26},{12,28},{14,30},{16,0},... | collective-permute-start | bytes 393224 | tf_op jit(solution)/shard_map/ppermute | solution.py:391
  57.3 9.4 %collective-permute-start.17 = (bf16[576,128]{1,0:T(8,128)(2,1)S(1)}, bf16[576,128]{1,0:T(8,128)(2,1)S(1)}, u32[]{:S(2)}, u32[]{:S(2)}) collective-permute-start(bf16[576,128]{1,0:T(8,128)(2,1)S(1)} %get-tuple-element.175), channel_id=1, source_target_pairs={{0,8},{2,10},{4,12},{6,14},{8,0},{10,2},{12,4},{14,6},{16,24},{18,... | collective-permute-start | bytes 442376 | tf_op jit(solution)/shard_map/ppermute | solution.py:391
  59.4 8.6 %collective-permute-start.18 = (bf16[768,128]{1,0:T(8,128)(2,1)S(1)}, bf16[768,128]{1,0:T(8,128)(2,1)S(1)}, u32[]{:S(2)}, u32[]{:S(2)}) collective-permute-start(bf16[768,128]{1,0:T(8,128)(2,1)S(1)} %get-tuple-element.184), channel_id=1, source_target_pairs={{0,1},{1,0},{2,3},{3,2},{4,5},{5,4},{6,7},{7,6},{8,9},{9,8},{10,11... | collective-permute-start | bytes 589832 | tf_op jit(solution)/shard_map/ppermute | solution.py:403
  62.5 7.6 %collective-permute-start.19 = (bf16[288,128]{1,0:T(8,128)(2,1)S(1)}, bf16[288,128]{1,0:T(8,128)(2,1)S(1)}, u32[]{:S(2)}, u32[]{:S(2)}) collective-permute-start(bf16[288,128]{1,0:T(8,128)(2,1)S(1)} %get-tuple-element.188), channel_id=1, source_target_pairs={{0,16},{2,18},{4,20},{6,22},{8,24},{10,26},{12,28},{14,30},{16,0},... | collective-permute-start | bytes 221192 | tf_op jit(solution)/shard_map/ppermute | solution.py:391
  63.4 8.7 %collective-permute-start.20 = (bf16[576,128]{1,0:T(8,128)(2,1)S(1)}, bf16[576,128]{1,0:T(8,128)(2,1)S(1)}, u32[]{:S(2)}, u32[]{:S(2)}) collective-permute-start(bf16[576,128]{1,0:T(8,128)(2,1)S(1)} %get-tuple-element.192), channel_id=1, source_target_pairs={{0,8},{2,10},{4,12},{6,14},{8,0},{10,2},{12,4},{14,6},{16,24},{18,... | collective-permute-start | bytes 442376 | tf_op jit(solution)/shard_map/ppermute | solution.py:391
  66.8 7.3 %collective-permute-start.21 = (bf16[288,128]{1,0:T(8,128)(2,1)S(1)}, bf16[288,128]{1,0:T(8,128)(2,1)S(1)}, u32[]{:S(2)}, u32[]{:S(2)}) collective-permute-start(bf16[288,128]{1,0:T(8,128)(2,1)S(1)} %get-tuple-element.201), channel_id=1, source_target_pairs={{0,16},{2,18},{4,20},{6,22},{8,24},{10,26},{12,28},{14,30},{16,0},... | collective-permute-start | bytes 221192 | tf_op jit(solution)/shard_map/ppermute | solution.py:391
  68.3 7.3 %collective-permute-start.24 = (bf16[576,128]{1,0:T(8,128)(2,1)S(1)}, bf16[576,128]{1,0:T(8,128)(2,1)S(1)}, u32[]{:S(2)}, u32[]{:S(2)}) collective-permute-start(bf16[576,128]{1,0:T(8,128)(2,1)S(1)} %get-tuple-element.205), channel_id=1, source_target_pairs={{0,8},{2,10},{4,12},{6,14},{8,0},{10,2},{12,4},{14,6},{16,24},{18,... | collective-permute-start | bytes 442376 | tf_op jit(solution)/shard_map/ppermute | solution.py:391
  72.2 6.1 %collective-permute-start.25 = (bf16[288,128]{1,0:T(8,128)(2,1)S(1)}, bf16[288,128]{1,0:T(8,128)(2,1)S(1)}, u32[]{:S(2)}, u32[]{:S(2)}) collective-permute-start(bf16[288,128]{1,0:T(8,128)(2,1)S(1)} %get-tuple-element.213), channel_id=1, source_target_pairs={{0,16},{2,18},{4,20},{6,22},{8,24},{10,26},{12,28},{14,30},{16,0},... | collective-permute-start | bytes 221192 | tf_op jit(solution)/shard_map/ppermute | solution.py:391
  74.1 8.3 %collective-permute-start.22 = (bf16[728,128]{1,0:T(8,128)(2,1)S(1)}, bf16[728,128]{1,0:T(8,128)(2,1)S(1)}, u32[]{:S(2)}, u32[]{:S(2)}) collective-permute-start(bf16[728,128]{1,0:T(8,128)(2,1)S(1)} %fusion.3), channel_id=1, source_target_pairs={{0,4},{2,6},{4,0},{6,2},{8,12},{10,14},{12,8},{14,10},{16,20},{18,... | collective-permute-start | bytes 559112 | tf_op jit(solution)/shard_map/ppermute | solution.py:391
  75.6 5.5 %collective-permute-start.26 = (bf16[288,128]{1,0:T(8,128)(2,1)S(1)}, bf16[288,128]{1,0:T(8,128)(2,1)S(1)}, u32[]{:S(2)}, u32[]{:S(2)}) collective-permute-start(bf16[288,128]{1,0:T(8,128)(2,1)S(1)} %get-tuple-element.225), channel_id=1, source_target_pairs={{0,16},{2,18},{4,20},{6,22},{8,24},{10,26},{12,28},{14,30},{16,0},... | collective-permute-start | bytes 221192 | tf_op jit(solution)/shard_map/ppermute | solution.py:391
  81.2 4.4 %collective-permute-start.27 = (bf16[288,128]{1,0:T(8,128)(2,1)S(1)}, bf16[288,128]{1,0:T(8,128)(2,1)S(1)}, u32[]{:S(2)}, u32[]{:S(2)}) collective-permute-start(bf16[288,128]{1,0:T(8,128)(2,1)S(1)} %pad_maximum_fusion.4), channel_id=1, source_target_pairs={{0,4},{2,6},{4,0},{6,2},{8,12},{10,14},{12,8},{14,10},{16,20},{18,... | collective-permute-start | bytes 221192 | tf_op jit(solution)/shard_map/ppermute | solution.py:391
  85.6 1.4 %collective-permute-start.28 = (bf16[576,128]{1,0:T(8,128)(2,1)S(1)}, bf16[576,128]{1,0:T(8,128)(2,1)S(1)}, u32[]{:S(2)}, u32[]{:S(2)}) collective-permute-start(bf16[576,128]{1,0:T(8,128)(2,1)S(1)} %pad_maximum_fusion.2), channel_id=1, source_target_pairs={{0,2},{2,0},{4,6},{6,4},{8,10},{10,8},{12,14},{14,12},{16,18},{18,... | collective-permute-start | bytes 442376 | tf_op jit(solution)/shard_map/ppermute | solution.py:391
  85.7 1.8 %collective-permute-start.23 = (bf16[1304,128]{1,0:T(8,128)(2,1)S(1)}, bf16[1304,128]{1,0:T(8,128)(2,1)S(1)}, u32[]{:S(2)}, u32[]{:S(2)}) collective-permute-start(bf16[1304,128]{1,0:T(8,128)(2,1)S(1)} %convert_dynamic-update-slice_fusion), channel_id=1, source_target_pairs={{0,2},{2,0},{4,6},{6,4},{8,10},{10,8},{12,14},{14,12},{16,18},{18,... | collective-permute-start | bytes 1001480 | tf_op jit(solution)/shard_map/ppermute | solution.py:391
